TPU v7x, 256 devices: a whole 4x4x8 slice. The times are simulated.
256 devices in a mesh: tm: 32 (over y, x, core), height: 8 (over z).
Axes of the slice: x: 4, y: 4, z: 8, core: 2. Of those that a mesh axis runs over, the one named last changes fastest.
Arguments:
- inputs: bfloat16 [64, 32, 64, 128], P('tm', 'height'), may hold values from -20 to 20
- gain_first: float32 [128], replicated, may hold values from 0.1 to 1.9
- shift_first: float32 [128], replicated, may hold values from -2 to 2
- weight_first: bfloat16 [3, 3, 3, 128, 128], replicated, may hold values from -0.109375 to 0.109375
- gain_second: float32 [128], replicated, may hold values from 0.1 to 1.9
- shift_second: float32 [128], replicated, may hold values from -2 to 2
- weight_second: bfloat16 [3, 3, 3, 128, 128], replicated, may hold values from -0.109375 to 0.109375
- upstream: bfloat16 [64, 32, 64, 128], P('tm', 'height'), may hold values from -12 to 12
Outputs:
- output: bfloat16 [64, 32, 64, 128], P('tm', 'height')
- input_grad: bfloat16 [64, 32, 64, 128], P('tm', 'height')
- weight_first_grad: float32 [3, 3, 3, 128, 128], replicated
- weight_second_grad: float32 [3, 3, 3, 128, 128], replicated
- gain_first_grad: float32 [128], replicated
- shift_first_grad: float32 [128], replicated
- gain_second_grad: float32 [128], replicated
- shift_second_grad: float32 [128], replicated
All inputs are finite; a program needn't handle non-finite values.
Results may differ from a plain program's by a relative error of at most 0.012.
Values may be sent and summed in bfloat16 or wider, within the bound.
A program may use at most 64 MiB of HBM per device.

v0:
```python
import jax
import jax.numpy as jnp
from jax import lax
from jax.sharding import PartitionSpec as P

C = 128
G = 32


epsilon = 1e-06


def from_behind(block, axis, distance):
    devices = range(lax.axis_size(axis))
    route = [(i - distance, i) for i in devices if i - distance in devices]
    return lax.ppermute(block, axis, route)


def extended_2(cells, sides, width):
    for axis, dim in sides:
        count = lax.axis_size(axis)
        ends = count - 1
        head = lax.slice_in_dim(cells, 0, width, axis=dim)
        tail = lax.slice_in_dim(cells, cells.shape[dim] - width, cells.shape[dim], axis=dim)
        cells = jnp.concatenate(
            [
                lax.ppermute(tail, axis, [(i, (i + 1) % count) for i in range(ends)]),
                cells,
                lax.ppermute(head, axis, [((i + 1) % count, i) for i in range(ends)]),
            ],
            axis=dim,
        )
    return cells


def group_sum(per_channel):
    return per_channel.reshape(G, -1).sum(axis=1)


def spread_groups(per_group):
    return jnp.repeat(per_group, C // G)


def group_members(values):
    return float(
        values.shape[0]
        * values.shape[1]
        * values.shape[2]
        * (C // G)
        * lax.axis_size("tm")
        * lax.axis_size("height")
    )


def norm_stats(values):
    members = group_members(values)
    totals = lax.psum(group_sum(jnp.sum(values, axis=(0, 1, 2))), ("tm", "height"))
    centre = totals / members
    deviate = values - spread_groups(centre)
    spread = (
        lax.psum(group_sum(jnp.sum(deviate * deviate, axis=(0, 1, 2))), ("tm", "height")) / members
    )
    return (spread_groups(centre), spread_groups(lax.rsqrt(spread + epsilon)))


def activate(values, centre, inverse, gain, offset):
    return jax.nn.silu((values - centre) * inverse * gain + offset)


def prior_slab(values):
    earlier = from_behind(values, "tm", 1)
    first_frame = jnp.broadcast_to(values[:1], earlier.shape)
    earlier = jnp.where(lax.axis_index("tm") == 0, first_frame, earlier)
    joined = jnp.concatenate([earlier, values], axis=0)
    return extended_2(joined, (("height", 1),), 1)


def later_slab(gradient):
    following = from_behind(gradient, "tm", -1)
    joined = jnp.concatenate([gradient, following], axis=0)
    return extended_2(joined, (("height", 1),), 1)


def pad_columns(extended):
    return jnp.pad(extended, ((0, 0), (0, 0), (1, 1), (0, 0)))


def tap_rows(padded, time_tap, row_tap, frames, row_count, width_cells):
    extended = padded[time_tap : time_tap + frames, row_tap : row_tap + row_count]
    pieces = [extended[:, :, column_tap : column_tap + width_cells] for column_tap in range(3)]
    return jnp.concatenate(pieces, axis=-1).reshape(frames * row_count * width_cells, -1)


def sweep(padded, weight, frames, row_count, width_cells):
    channels = weight.shape[-1]
    running = jnp.zeros((frames * row_count * width_cells, channels), jnp.float32)
    for time_tap in range(3):
        for row_tap in range(3):
            patches = tap_rows(padded, time_tap, row_tap, frames, row_count, width_cells)
            running = running + jnp.dot(
                patches,
                weight[time_tap, row_tap].reshape(-1, channels),
                preferred_element_type=jnp.float32,
            )
    return running


def weight_terms(padded, gradient_rows, frames, row_count, width_cells):
    pieces = []
    for time_tap in range(3):
        for row_tap in range(3):
            patches = tap_rows(padded, time_tap, row_tap, frames, row_count, width_cells)
            pieces.append(
                lax.dot_general(
                    patches,
                    gradient_rows,
                    (((0,), (0,)), ((), ())),
                    preferred_element_type=jnp.float32,
                )
            )
    channels = gradient_rows.shape[-1]
    return jnp.stack(pieces).reshape(3, 3, 3, channels, channels)


def norm_conv(values, gain, offset, weight):
    frames, row_count, width_cells, channels = values.shape
    local_vals = values.astype(jnp.float32)
    centre, inverse = norm_stats(local_vals)
    activated = activate(local_vals, centre, inverse, gain, offset).astype(jnp.bfloat16)
    extended = prior_slab(activated)
    padded = pad_columns(extended)
    result = sweep(padded, weight, frames, row_count, width_cells)
    return (result, padded, local_vals.reshape(-1, channels), centre, inverse)


def back_conv(gradient, weight, padded):
    frames, row_count, width_cells, channels = gradient.shape
    weight_grad = weight_terms(
        padded, gradient.reshape(-1, channels), frames, row_count, width_cells
    )
    grad_pad = pad_columns(later_slab(gradient))
    flipped = jnp.transpose(jnp.flip(weight, (0, 1, 2)), (0, 1, 2, 4, 3))
    input_grad = sweep(grad_pad, flipped, frames, row_count, width_cells)

    def folded():
        prefixed = jnp.concatenate([jnp.zeros_like(grad_pad[:2]), grad_pad[:2]], axis=0)
        halves = sweep(prefixed, flipped, 2, row_count, width_cells).reshape(
            2, row_count * width_cells, channels
        )
        return halves[0] + halves[1]

    def nothing():
        return jnp.zeros((row_count * width_cells, channels), jnp.float32)

    extras = lax.cond(lax.axis_index("tm") == 0, folded, nothing)
    input_grad = input_grad.at[: row_count * width_cells].add(extras)
    return (input_grad, weight_grad)


def norm_back(act_grad, values, centre, inverse, gain, offset, members):
    normed = (values - centre) * inverse
    affine = normed * gain + offset
    sigmoid_val = jax.nn.sigmoid(affine)
    pre_grad = act_grad * sigmoid_val * (1.0 + affine * (1.0 - sigmoid_val))
    gain_grad, offset_grad = lax.psum(
        (jnp.sum(pre_grad * normed, axis=0), jnp.sum(pre_grad, axis=0)), ("tm", "height")
    )
    mean_grad = spread_groups(group_sum(gain * offset_grad) / members)
    mean_cross = spread_groups(group_sum(gain * gain_grad) / members)
    value_grad = inverse * (pre_grad * gain - mean_grad - normed * mean_cross)
    return (value_grad, gain_grad, offset_grad)


def body(
    inputs,
    gain_first,
    shift_first,
    weight_first,
    gain_second,
    shift_second,
    weight_second,
    upstream,
):
    shape = inputs.shape
    members = group_members(inputs)
    hidden_raw, padded_one, values_one, centre_one, inverse_one = norm_conv(
        inputs, gain_first, shift_first, weight_first
    )
    hidden = hidden_raw.astype(jnp.bfloat16).reshape(shape)
    branch, padded_two, values_two, centre_two, inverse_two = norm_conv(
        hidden, gain_second, shift_second, weight_second
    )
    grad_rows = upstream.reshape(-1, shape[-1]).astype(jnp.float32)
    output = (values_one + branch).astype(jnp.bfloat16).reshape(shape)
    act_grad_two, second_local = back_conv(upstream, weight_second, padded_two)
    value_two, gain_second_grad, shift_second_grad = norm_back(
        act_grad_two, values_two, centre_two, inverse_two, gain_second, shift_second, members
    )
    hidden_grad = value_two.astype(jnp.bfloat16).reshape(shape)
    act_grad_one, first_local = back_conv(hidden_grad, weight_first, padded_one)
    value_one, gain_first_grad, shift_first_grad = norm_back(
        act_grad_one, values_one, centre_one, inverse_one, gain_first, shift_first, members
    )
    input_grad = (grad_rows + value_one).astype(jnp.bfloat16).reshape(shape)
    first_total, second_total = lax.psum((first_local, second_local), ("tm", "height"))
    return (
        output,
        input_grad,
        first_total,
        second_total,
        gain_first_grad,
        shift_first_grad,
        gain_second_grad,
        shift_second_grad,
    )


def solution(mesh):
    placed = (
        P("tm", "height", None, None),
        P(),
        P(),
        P(),
        P(),
        P(),
        P(),
        P("tm", "height", None, None),
    )
    return jax.shard_map(
        body,
        mesh=mesh,
        in_specs=placed,
        out_specs=(
            P("tm", "height", None, None),
            P("tm", "height", None, None),
            P(),
            P(),
            P(),
            P(),
            P(),
            P(),
        ),
        check_vma=False,
    )
```

profile of v0, /device:TPU:1, one launch (start us, length us, event | category | flops | bytes accessed | tf_op | source)
XLA Modules:
  0.0 840.1 jit_solution(2048835274261908640)
XLA Ops:
  8.5 81.4 %psum.70 = f32[32]{0:T(128)S(1)} all-reduce(f32[32]{0:T(128)S(1)} %reduce_sum.145), channel_id=1, replica_groups=mesh['tm'=32,'height'=8] {'tm','height'}, use_global_device_ids=true, to_apply=%region_2.0 | all-reduce | flops 32 | bytes 256 | tf_op jit(solution)/shard_map/psum | solution.py:57
  91.3 72.4 %psum.71 = f32[32]{0:T(128)S(1)} all-reduce(f32[32]{0:T(128)S(1)} %reduce_sum.147), channel_id=1, replica_groups=mesh['tm'=32,'height'=8] {'tm','height'}, use_global_device_ids=true, to_apply=%region_5.0 | all-reduce | flops 32 | bytes 256 | tf_op jit(solution)/shard_map/psum | solution.py:61
  165.0 3.0 collective-permute-start
  168.0 2.1 collective-permute-start.6
  170.1 2.2 fusion.73
  172.3 1.7 copy.18
  174.9 1.4 copy.19
  179.3 1.3 collective-permute-start.2
  180.6 4.3 collective-permute-start.1
  192.6 4.0 collective-permute-start.7
  196.6 78.5 %psum.72 = f32[32]{0:T(128)S(1)} all-reduce(f32[32]{0:T(128)S(1)} %reduce_sum.149), channel_id=1, replica_groups=mesh['tm'=32,'height'=8] {'tm','height'}, use_global_device_ids=true, to_apply=%region_8.9 | all-reduce | flops 32 | bytes 256 | tf_op jit(solution)/shard_map/psum | solution.py:57
  275.8 1.5 fusion.76
  277.2 72.3 %psum.73 = f32[32]{0:T(128)S(1)} all-reduce(f32[32]{0:T(128)S(1)} %reduce_sum.151), channel_id=1, replica_groups=mesh['tm'=32,'height'=8] {'tm','height'}, use_global_device_ids=true, to_apply=%region_11.12 | all-reduce | flops 32 | bytes 256 | tf_op jit(solution)/shard_map/psum | solution.py:61
  349.9 3.0 collective-permute-start.3
  352.9 1.4 fusion.44
  359.9 1.7 fusion.63
  361.6 1.8 fusion.66
  363.4 74.9 %all-reduce.9 = (f32[128]{0:T(128)S(1)}, f32[128]{0:T(128)S(1)}) all-reduce(f32[128]{0:T(128)S(1)} %get-tuple-element.53, f32[128]{0:T(128)S(1)} %get-tuple-element.52), channel_id=1, replica_groups=mesh['tm'=32,'height'=8] {'tm','height'}, use_global_device_ids=true, to_apply=%region_18.19 | all-reduce | flops 256 | bytes 2048 | tf_op jit(solution)/shard_map/psum | solution.py:165
  440.6 2.7 collective-permute-start.9
  443.3 1.3 fusion.28
  448.5 4.0 collective-permute-start.10
  453.5 1.3 collective-permute-start.5
  454.8 4.0 collective-permute-start.4
  460.4 1.4 fusion.77
  468.6 1.4 convolution_add_fusion.23
  473.5 78.4 %all-reduce.8 = (f32[128]{0:T(128)S(1)}, f32[128]{0:T(128)S(1)}) all-reduce(f32[128]{0:T(128)S(1)} %get-tuple-element.51, f32[128]{0:T(128)S(1)} %get-tuple-element.50), channel_id=1, replica_groups=mesh['tm'=32,'height'=8] {'tm','height'}, use_global_device_ids=true, to_apply=%region_26.27 | all-reduce | flops 256 | bytes 2048 | tf_op jit(solution)/shard_map/psum | solution.py:165
  553.2 1.9 pad_maximum_fusion.27
  556.5 1.4 fusion.18
  565.9 1.3 convolution_add_fusion.39
  567.2 1.4 fusion.56
  571.6 257.4 %all-reduce.13.cloned.1.call-done = (f32[3,3,3,128,128]{4,3,2,1,0:T(8,128)}, f32[3,3,3,128,128]{4,3,2,1,0:T(8,128)}) async-done(((f32[3,3,3,128,128]{4,3,2,1,0:T(8,128)}, f32[3,3,3,128,128]{4,3,2,1,0:T(8,128)}), (f32[3,3,3,128,128]{4,3,2,1,0:T(8,128)}, f32[3,3,3,128,128]{4,3,2,1,0:T(8,128)})) %all-reduce.13.cloned.1.call-update) | async-done | bytes 3538960 | tf_op jit(solution)/shard_map/psum | solution.py:205
  829.0 3.0 copy.54
  (412 shorter events, 54.5 us)
Async XLA Ops:
  7.2 165.1 %copy-start.1 = (bf16[3,3,3,128,128]{4,3,2,1,0:T(8,128)(2,1)S(1)}, bf16[3,3,3,128,128]{4,3,2,1,0:T(8,128)(2,1)}, u32[]{:S(2)}) copy-start(bf16[3,3,3,128,128]{4,3,2,1,0:T(8,128)(2,1)} %param.22) | copy-start | bytes 2654212
  7.2 821.9 %all-reduce.13.cloned.1.call-start = ((), (), s32[]{:S(2)}) async-start(), calls=%async_computation | async-start | bytes 7077888 | tf_op jit(solution)/shard_map/psum | solution.py:205
  90.1 83.9 %copy-start.108 = (f32[128]{0:T(128)}, f32[128]{0:T(128)S(1)}, u32[]{:S(2)}) copy-start(f32[128]{0:T(128)S(1)} %sub.77) | copy-start | bytes 1540
  163.9 10.0 %copy-start.112 = (f32[128]{0:T(128)}, f32[128]{0:T(128)S(1)}, u32[]{:S(2)}) copy-start(f32[128]{0:T(128)S(1)} %mul.163) | copy-start | bytes 1540
  165.0 9.0 %copy-start.2 = (bf16[3,3,3,128,128]{4,3,2,1,0:T(8,128)(2,1)S(1)}, bf16[3,3,3,128,128]{4,3,2,1,0:T(8,128)(2,1)}, u32[]{:S(2)}) copy-start(bf16[3,3,3,128,128]{4,3,2,1,0:T(8,128)(2,1)} %param.19) | copy-start | bytes 2654212
  165.0 13.3 %collective-permute-start = (bf16[2,4,64,128]{3,2,1,0:T(8,128)(2,1)S(1)}, bf16[2,4,64,128]{3,2,1,0:T(8,128)(2,1)}, u32[]{:S(2)}, u32[]{:S(2)}) collective-permute-start(bf16[2,4,64,128]{3,2,1,0:T(8,128)(2,1)S(1)} %multiply_convert_fusion.2), channel_id=1, source_target_pairs={{0,8},{8,16},{16,24},{24,32},{32,40},{40,48},{48,56},{56,64},{64,7... | collective-permute-start | bytes 393224 | tf_op jit(solution)/shard_map/ppermute | solution.py:16
  168.0 16.9 %collective-permute-start.6 = (bf16[2,4,64,128]{3,2,1,0:T(8,128)(2,1)}, bf16[2,4,64,128]{3,2,1,0:T(8,128)(2,1)S(1)}, u32[]{:S(2)}, u32[]{:S(2)}) collective-permute-start(bf16[2,4,64,128]{3,2,1,0:T(8,128)(2,1)} %param.23), channel_id=1, source_target_pairs={{8,0},{16,8},{24,16},{32,24},{40,32},{48,40},{56,48},{64,56},{72,6... | collective-permute-start | bytes 393224 | tf_op jit(solution)/shard_map/ppermute | solution.py:16
  179.3 7.6 collective-permute-start.2
  180.6 6.3 collective-permute-start.1
  185.6 90.0 %collective-permute-start.8 = (bf16[4,1,64,128]{3,2,1,0:T(8,128)(2,1)}, bf16[4,1,64,128]{3,2,1,0:T(8,128)(2,1)S(1)}, u32[]{:S(2)}, u32[]{:S(2)}) collective-permute-start(bf16[4,1,64,128]{3,2,1,0:T(8,128)(2,1)} %get-tuple-element.264), channel_id=1, source_target_pairs={{1,0},{2,1},{3,2},{4,3},{5,4},{6,5},{7,6},{9,8},{10,9},{11,10},{12... | collective-permute-start | bytes 196616 | tf_op jit(solution)/shard_map/ppermute | solution.py:29
  192.6 83.0 %collective-permute-start.7 = (bf16[4,1,64,128]{3,2,1,0:T(8,128)(2,1)S(1)}, bf16[4,1,64,128]{3,2,1,0:T(8,128)(2,1)S(1)}, u32[]{:S(2)}, u32[]{:S(2)}) collective-permute-start(bf16[4,1,64,128]{3,2,1,0:T(8,128)(2,1)S(1)} %copy-done.107), channel_id=1, source_target_pairs={{0,1},{1,2},{2,3},{3,4},{4,5},{5,6},{6,7},{8,9},{9,10},{10,11},{11... | collective-permute-start | bytes 196616 | tf_op jit(solution)/shard_map/ppermute | solution.py:27
  275.7 74.0 %copy-start.110 = (f32[128]{0:T(128)S(1)}, f32[128]{0:T(128)}, u32[]{:S(2)}) copy-start(f32[128]{0:T(128)} %param.20) | copy-start | bytes 1540
  275.7 74.0 %copy-start.114 = (f32[128]{0:T(128)S(1)}, f32[128]{0:T(128)}, u32[]{:S(2)}) copy-start(f32[128]{0:T(128)} %param.21) | copy-start | bytes 1540
  349.9 102.6 %collective-permute-start.3 = (bf16[2,4,64,128]{3,2,1,0:T(8,128)(2,1)S(1)}, bf16[2,4,64,128]{3,2,1,0:T(8,128)(2,1)}, u32[]{:S(2)}, u32[]{:S(2)}) collective-permute-start(bf16[2,4,64,128]{3,2,1,0:T(8,128)(2,1)S(1)} %multiply_convert_fusion.1), channel_id=1, source_target_pairs={{0,8},{8,16},{16,24},{24,32},{32,40},{40,48},{48,56},{56,64},{64,7... | collective-permute-start | bytes 393224 | tf_op jit(solution)/shard_map/ppermute | solution.py:16
  359.8 80.4 %copy-start.5 = (bf16[2,4,64,384]{3,2,1,0:T(8,128)(2,1)S(1)}, bf16[2,4,64,384]{3,2,1,0:T(8,128)(2,1)}, u32[]{:S(2)}) copy-start(bf16[2,4,64,384]{3,2,1,0:T(8,128)(2,1)} %copy-done.4) | copy-start | bytes 1179652
  359.8 84.8 %copy-start.7 = (bf16[2,4,64,384]{3,2,1,0:T(8,128)(2,1)S(1)}, bf16[2,4,64,384]{3,2,1,0:T(8,128)(2,1)}, u32[]{:S(2)}) copy-start(bf16[2,4,64,384]{3,2,1,0:T(8,128)(2,1)} %copy-done.6) | copy-start | bytes 1179652
  361.6 83.4 %copy-start.11 = (bf16[2,4,64,384]{3,2,1,0:T(8,128)(2,1)S(1)}, bf16[2,4,64,384]{3,2,1,0:T(8,128)(2,1)}, u32[]{:S(2)}) copy-start(bf16[2,4,64,384]{3,2,1,0:T(8,128)(2,1)} %copy-done.10) | copy-start | bytes 1179652
  438.3 6.9 copy-start.116
  438.3 7.0 copy-start.117
  439.2 6.1 copy-start.17
  440.3 5.4 copy-start.9
  440.6 5.4 copy-start.15
  440.6 6.6 collective-permute-start.9
  446.9 11.8 %copy-start.19 = (f32[9,384,128]{2,1,0:T(8,128)}, f32[9,384,128]{2,1,0:T(8,128)S(1)}, u32[]{:S(2)}) copy-start(f32[9,384,128]{2,1,0:T(8,128)S(1)} %fusion.21) | copy-start | bytes 5308420
  447.2 11.6 %collective-permute-start.11 = (bf16[4,1,64,128]{3,2,1,0:T(8,128)(2,1)S(1)}, bf16[4,1,64,128]{3,2,1,0:T(8,128)(2,1)S(1)}, u32[]{:S(2)}, u32[]{:S(2)}) collective-permute-start(bf16[4,1,64,128]{3,2,1,0:T(8,128)(2,1)S(1)} %get-tuple-element.257), channel_id=1, source_target_pairs={{1,0},{2,1},{3,2},{4,3},{5,4},{6,5},{7,6},{9,8},{10,9},{11,10},{12... | collective-permute-start | bytes 196616 | tf_op jit(solution)/shard_map/ppermute | solution.py:29
  448.5 10.3 %collective-permute-start.10 = (bf16[4,1,64,128]{3,2,1,0:T(8,128)(2,1)S(1)}, bf16[4,1,64,128]{3,2,1,0:T(8,128)(2,1)S(1)}, u32[]{:S(2)}, u32[]{:S(2)}) collective-permute-start(bf16[4,1,64,128]{3,2,1,0:T(8,128)(2,1)S(1)} %get-tuple-element.256), channel_id=1, source_target_pairs={{0,1},{1,2},{2,3},{3,4},{4,5},{5,6},{6,7},{8,9},{9,10},{10,11},{11... | collective-permute-start | bytes 196616 | tf_op jit(solution)/shard_map/ppermute | solution.py:27
  453.5 6.6 collective-permute-start.5
  454.8 5.5 collective-permute-start.4
  472.7 82.4 %copy-start.21 = (f32[9,384,128]{2,1,0:T(8,128)S(1)}, f32[9,384,128]{2,1,0:T(8,128)}, u32[]{:S(2)}) copy-start(f32[9,384,128]{2,1,0:T(8,128)} %fusion.20) | copy-start | bytes 5308420
  551.9 6.1 copy-start.118
  551.9 6.1 copy-start.119
  553.2 4.7 copy-start.68
  (101 other events, 167.9 us)
Sparse Core Ops, SparseCore 0:
  565.8 263.1 all-reduce.12
where the time goes:
time: 842 us; the launch traced here: 840 us
  blocking collectives  458 us (54%)
  waiting for transfers between devices  258 us (31%)
  starting transfers between devices  32.2 us (4%)
  local copies, waits for them, and re-layouts  29.4 us (3%)
  matrix products  23.7 us (3%)
  other arithmetic  22.3 us (3%)
  between operations  16.4 us (2%)
    psum x1, waiting for transfers between devices, body(): lax.psum((first_local, second_local), ('tm', 'height'))  257 us
    psum x2, blocking collectives, norm_stats(): lax.psum(group_sum(jnp.sum(values, axis=(0, 1, 2))), ('tm', 'height'))  160 us
    psum x2, blocking collectives, norm_back(): lax.psum((jnp.sum(pre_grad * normed, axis=0), jnp.sum(pre_grad, axis=0)),...  153 us
    psum x2, blocking collectives, norm_stats(): lax.psum(group_sum(jnp.sum(deviate * deviate, axis=(0, 1, 2))), ('tm', 'h...  145 us
  transfers between devices with their start and end apart: 13, of which 3 were waited for; matrix products, arithmetic and copies ran while one was open for 4% of the time, Pallas kernels for 0%

commit v1 on v0

v1 whole, which is shorter than its diff:
```python
import functools
import types

import jax
import jax.numpy as jnp
from jax import lax
from jax.experimental import pallas as pl
from jax.experimental.pallas import tpu as pltpu
from jax.sharding import PartitionSpec as P

C = 128
G = 32
MEMBERS = C // G
EPSILON = 1e-06
MESH = pl.DeviceIdType.MESH
F32 = jnp.float32
BF16 = jnp.bfloat16


def plan_of(tm, height, frames, rows, columns):
    s = types.SimpleNamespace()
    s.tm, s.nz = tm, height
    s.nyx = tm // 2
    s.nx = 4 if s.nyx >= 16 else 2
    s.ny = s.nyx // s.nx
    s.frames, s.rows, s.columns = frames, rows, columns
    s.stages = (s.nz, 2 * s.nx, s.ny)
    s.taps = 28
    s.half = s.taps * C // 2
    s.parts = ((("y", "x", 1024), ("x", "y", s.half - 1024)), (("x", "y", s.half),))
    s.size = {"y": s.ny, "x": s.nx}
    s.kept = s.half // s.nyx
    s.z_rows = 16 * -(-s.kept // 16 // s.nz)
    return s


def bundle(sem, ref):
    pltpu.make_async_copy(ref, ref, sem).wait()


def group_total(row):
    lane = lax.broadcasted_iota(jnp.int32, row.shape, 1)
    for step in (1, 2):
        ahead = pltpu.roll(row, C - step, 1)
        behind = pltpu.roll(row, step, 1)
        row = row + jnp.where(lane & step == 0, ahead, behind)
    return row


def wrap(i, n):
    return jnp.where(i >= n, i - n, i)


def sigmoid(u):
    return 1.0 / (1.0 + jnp.exp(-u))


class Place:
    def __init__(self, s):
        self.s = s
        self.tm = tm = lax.axis_index("tm")
        self.z = z = lax.axis_index("height")
        self.core = core = tm % 2
        self.yx = yx = tm // 2
        self.x = yx % s.nx
        self.y = yx // s.nx
        self.mate_tm = mate_tm = tm + 1 - 2 * core
        self.z_ring = z_ring = [z] + [wrap(z + d, s.nz) for d in range(1, s.nz)]
        self.x_ring = [self.x] + [wrap(self.x + d, s.nx) for d in range(1, s.nx)]
        self.y_ring = [self.y] + [wrap(self.y + d, s.ny) for d in range(1, s.ny)]
        self.rings = {"y": self.y_ring, "x": self.x_ring}
        self.row = [self.tm_of(self.y, q, core) for q in self.x_ring]
        self.column = [self.tm_of(q, self.x, core) for q in self.y_ring]
        self.lines = {"y": self.column, "x": self.row}
        self.groups = (
            (z, [(tm, q) for q in z_ring[1:]]),
            (self.x * 2 + core, [(mate_tm, z)] + [(q, z) for q in self.row[1:]]
             + [(q + 1 - 2 * core, z) for q in self.row[1:]]),
            (self.y, [(q, z) for q in self.column[1:]]),
        )
        self.tm_next, self.tm_prev = wrap(tm + 1, s.tm), wrap(tm + s.tm - 1, s.tm)
        self.z_next, self.z_prev = z_ring[1], z_ring[-1]
        self.partners = [peer for _, peers in self.groups for peer in peers]
        self.partners = self.partners + [
            (t, q) for t in (self.tm_next, self.tm_prev) for q in (z, self.z_next, self.z_prev)
        ]

    def tm_of(self, y, x, core):
        return (y * self.s.nx + x) * 2 + core

    def greet(self):
        barrier = pltpu.get_barrier_semaphore()
        for partner in self.partners:
            pl.semaphore_signal(barrier, inc=1, device_id=partner, device_id_type=MESH)

    def meet(self):
        pl.semaphore_wait(pltpu.get_barrier_semaphore(), len(self.partners))

    def own_block(self, ref, lo):
        return ref.at[pl.ds(lo, self.s.frames), pl.ds(1, self.s.rows)]

    def own(self, ref):
        return ref[...].astype(F32).reshape(-1, C)

    def bind(self, ar, ar_send, ar_recv, halo_send, halo_recv):
        self.ar, self.ar_send, self.ar_recv = ar, ar_send, ar_recv
        self.halo_send, self.halo_recv = halo_send, halo_recv

    def ar_start(self, k, stage, payload):
        i = 3 * k + stage
        slot, peers = self.groups[stage]
        self.ar[i, slot, 0:1] = payload[0]
        self.ar[i, slot, 1:2] = payload[1]
        for peer in peers:
            pltpu.make_async_remote_copy(
                src_ref=self.ar.at[i, slot],
                dst_ref=self.ar.at[i, slot],
                send_sem=self.ar_send.at[i],
                recv_sem=self.ar_recv.at[i],
                device_id=peer,
                device_id_type=MESH,
            ).start()

    def ar_wait(self, k, stage):
        i = 3 * k + stage
        n = self.s.stages[stage]
        bundle(self.ar_recv.at[i], self.ar.at[i, pl.ds(0, n - 1)])
        parts = [self.ar[i, j] for j in range(n)]
        return [p[0:1] for p in parts], [p[1:2] for p in parts]

    def ar_sent(self, k):
        for stage, n in enumerate(self.s.stages):
            i = 3 * k + stage
            bundle(self.ar_send.at[i], self.ar.at[i, pl.ds(0, n - 1)])

    def local_count(self):
        return float(self.s.frames * self.s.rows * self.s.columns * MEMBERS)

    def local_stats(self, v):
        centre = group_total(jnp.sum(v, axis=0, keepdims=True)) / self.local_count()
        spread = group_total(jnp.sum((v - centre) ** 2, axis=0, keepdims=True))
        return centre, spread

    def join_stats(self, parts, count):
        means, spreads = parts
        centre = sum(means) / float(len(means))
        spread = sum(spreads) + count * sum((mean - centre) ** 2 for mean in means)
        return centre, spread

    def stats_stage(self, k, stage):
        count = self.local_count()
        for n in self.s.stages[:stage]:
            count = count * n
        joined = self.join_stats(self.ar_wait(k, stage), count)
        if stage < 2:
            return self.ar_start(k, stage + 1, joined)
        centre, spread = joined
        return centre, lax.rsqrt(spread / (count * self.s.stages[stage]) + EPSILON)

    def sums_stage(self, k, stage):
        first, second = self.ar_wait(k, stage)
        totals = sum(first), sum(second)
        return totals if stage == 2 else self.ar_start(k, stage + 1, totals)

    def halo_start(self, q, ref, ahead):
        F, R, z = self.s.frames, self.s.rows, self.z
        target = self.tm_next if ahead else self.tm_prev
        far, near = (0, 2) if ahead else (2, 0)
        frames = pl.ds(near, F)
        everything = ref.at[frames, pl.ds(1, R)]
        top, bottom = ref.at[frames, pl.ds(1, 1)], ref.at[frames, pl.ds(R, 1)]
        copies = [
            (everything, ref.at[pl.ds(far, F), pl.ds(1, R)], (target, z)),
            (top, ref.at[pl.ds(near, F), pl.ds(R + 1, 1)], (self.tm, self.z_prev)),
            (bottom, ref.at[pl.ds(near, F), pl.ds(0, 1)], (self.tm, self.z_next)),
            (top, ref.at[pl.ds(far, F), pl.ds(R + 1, 1)], (target, self.z_prev)),
            (bottom, ref.at[pl.ds(far, F), pl.ds(0, 1)], (target, self.z_next)),
        ]
        for piece, place, device in copies:
            pltpu.make_async_remote_copy(
                src_ref=piece,
                dst_ref=place,
                send_sem=self.halo_send.at[q],
                recv_sem=self.halo_recv.at[q],
                device_id=device,
                device_id_type=MESH,
            ).start()

    def halo_bytes(self, sem, ref):
        F, R = self.s.frames, self.s.rows
        bundle(sem, ref.at[pl.ds(0, F + 2), pl.ds(0, F * (R + 4) // (F + 2))])

    def halo_wait(self, q, ref):
        self.halo_bytes(self.halo_recv.at[q], ref)

    def halo_sent(self, q, ref):
        self.halo_bytes(self.halo_send.at[q], ref)


def blank_next(place, ref):
    F = place.s.frames

    @pl.when(place.tm == place.s.tm - 1)
    def _():
        ref[F : F + 2] = jnp.zeros((2,) + ref.shape[1:], ref.dtype)


def copy_first(place, ref):
    @pl.when(place.tm == 0)
    def _():
        ref[0] = ref[2]
        ref[1] = ref[2]


def kernel(
    s,
    x_hbm,
    u_hbm,
    w1_hbm,
    w2_hbm,
    g1_hbm,
    s1_hbm,
    g2_hbm,
    s2_hbm,
    out_hbm,
    ig_hbm,
    wo1_hbm,
    wo2_hbm,
    gg1_hbm,
    sg1_hbm,
    gg2_hbm,
    sg2_hbm,
    w1_ref,
    w2_ref,
    vectors,
    out_ref,
    ig_ref,
    wo,
    results,
    xe,
    ue,
    he,
    ge,
    a1,
    a2,
    g3,
    dact,
    pre_buf,
    ar,
    wg,
    r1,
    p1,
    p3,
    r4,
    zt,
    arrivals,
    ar_send,
    ar_recv,
    halo_send,
    halo_recv,
    w_send,
    w_recv,
    load_sem,
    store_sem,
):
    F, R, W = s.frames, s.rows, s.columns
    E, RE = F + 2, R + 2
    cells = R * W
    place = Place(s)
    place.bind(ar, ar_send, ar_recv, halo_send, halo_recv)
    tm, z, x, y, core = place.tm, place.z, place.x, place.y, place.core
    mate_tm, z_ring = place.mate_tm, place.z_ring

    x_ref, u_ref = place.own_block(xe, 2), place.own_block(ue, 0)
    loads = [
        (x_hbm, x_ref),
        (u_hbm, u_ref),
        (w1_hbm, w1_ref),
        (w2_hbm, w2_ref),
        (g1_hbm, vectors.at[0]),
        (s1_hbm, vectors.at[1]),
        (g2_hbm, vectors.at[2]),
        (s2_hbm, vectors.at[3]),
    ]
    loads = [pltpu.make_async_copy(a, b, load_sem.at[i]) for i, (a, b) in enumerate(loads)]
    for load in loads:
        load.start()
    place.greet()

    def shifted(v, dst, f):
        column = lax.broadcasted_iota(jnp.int32, v.shape, 0) & (W - 1)
        left = jnp.where(column == 0, 0.0, pltpu.roll(v, 1, 0))
        right = jnp.where(column == W - 1, 0.0, pltpu.roll(v, RE * W - 1, 0))
        for k, piece in enumerate((left, v, right)):
            dst[f, :, :, k * C : (k + 1) * C] = piece.astype(BF16).reshape(RE, W, C)

    def blank_rows(dst):
        blank = jnp.zeros((E, 1) + dst.shape[2:], dst.dtype)

        @pl.when(z == 0)
        def _():
            dst[:, 0:1] = blank

        @pl.when(z == s.nz - 1)
        def _():
            dst[:, R + 1 : R + 2] = blank

    def build_act(src, dst, stats, gain, shift):
        centre, inverse = stats
        scale = inverse * gain

        def frame(f, carry):
            v = src[f].astype(F32).reshape(RE * W, C)
            affine = (v - centre) * scale + shift
            shifted(affine * sigmoid(affine), dst, f)
            return carry

        lax.fori_loop(0, E, frame, 0)
        blank_rows(dst)

    def build_grad(src):
        def frame(f, carry):
            shifted(src[f].astype(F32).reshape(RE * W, C), g3, f)
            return carry

        lax.fori_loop(0, E, frame, 0)
        blank_rows(g3)

    def dot(a, b):
        return jnp.dot(a, b, preferred_element_type=F32)

    def dot_lanes(a, b):
        return lax.dot_general(a, b, (((1,), (1,)), ((), ())), preferred_element_type=F32)

    def patches(src, f):
        return jnp.concatenate([src[f, j : j + R].reshape(cells, 3 * C) for j in range(3)], axis=1)

    def conv(src, weight):
        taps = [weight[9 * i : 9 * i + 9].reshape(9 * C, C) for i in range(3)]
        first = dot(patches(src, 0), taps[0])
        second = None
        for f in (1, 2):
            both = dot(patches(src, f), jnp.concatenate([taps[f], taps[f - 1]], axis=1))
            first = first + both[:, :C]
            second = both[:, C:] if second is None else second + both[:, C:]
        return first, second + dot(patches(src, 3), taps[2])

    def back_conv(src, weight):
        def flipped(i):
            return jnp.concatenate([weight[9 * i + 8 - jk] for jk in range(9)], axis=1)

        def pair(i):
            return jnp.concatenate([flipped(i), flipped(i + 1)], axis=0)

        first = dot_lanes(patches(src, 0), flipped(2))
        second = None
        for f in (1, 2):
            both = dot_lanes(patches(src, f), pair(2 - f))
            first = first + both[:, :C]
            second = both[:, C:] if second is None else second + both[:, C:]
        dact[0] = first
        dact[1] = second + dot_lanes(patches(src, 3), flipped(0))

        @pl.when(tm == 0)
        def _():
            both = dot_lanes(patches(src, 0), pair(0))
            dact[0] += both[:, :C] + both[:, C:] + dot_lanes(patches(src, 1), flipped(0))

    def weight_grad(act, grad, q):
        turned = [grad[f].reshape(cells, C).T for f in range(F)]
        both = jnp.concatenate(turned, axis=0)
        wg[q, 14 * C : 15 * C, :] = jnp.zeros((C, C), BF16)
        mate = (mate_tm, z)

        def row_tap(j, base):
            window = [act[f, pl.ds(j, R)].reshape(cells, 3 * C) for f in range(E)]
            one, two = dot(both, window[1]), dot(both, window[2])
            sums = (
                dot(turned[0], window[0]) + one[C:],
                one[:C] + two[C:],
                two[:C] + dot(turned[1], window[3]),
            )
            for i, total in enumerate(sums):
                total = total.astype(BF16)
                for k in range(3):
                    at = 3 * i + k
                    lo = base(at) * C
                    wg[q, pl.ds(pl.multiple_of(lo, C), C), :] = total[:, k * C : (k + 1) * C].T

        def send(i, src, dst, taps):
            pltpu.make_async_remote_copy(
                src_ref=wg.at[q, pl.ds(pl.multiple_of(src * C, C), taps * C)],
                dst_ref=r1.at[q, pl.ds(pl.multiple_of(dst * C, C), taps * C)],
                send_sem=w_send.at[q, i],
                recv_sem=w_recv.at[q, i],
                device_id=mate,
                device_id_type=MESH,
            ).start()

        row_tap(2 - 2 * core, lambda at: (1 - core) * 19 + at)
        send(0, (1 - core) * 19, (1 - core) * 5, 9)
        row_tap(1, lambda at: 9 + at if at < 5 else 10 + at)
        send(1, 14 - core * 5, core * 9, 5)
        row_tap(2 * core, lambda at: core * 19 + at)

    def norm_back_sums(values, stats, gain, shift):
        centre, inverse = stats
        total_cross = jnp.zeros((1, C), F32)
        total = jnp.zeros((1, C), F32)
        for f in range(F):
            normed = (values[f].astype(F32).reshape(cells, C) - centre) * inverse
            affine = normed * gain + shift
            sig = sigmoid(affine)
            pre = dact[f] * sig * (1.0 + affine * (1.0 - sig))
            pre_buf[f] = pre
            total_cross += jnp.sum(pre * normed, axis=0, keepdims=True)
            total += jnp.sum(pre, axis=0, keepdims=True)
        return total_cross, total

    def norm_back_value(values, stats, gain, sums, f):
        centre, inverse = stats
        gain_grad, shift_grad = sums
        members = float(F * cells * MEMBERS * s.tm * s.nz)
        mean_grad = group_total(gain * shift_grad) / members
        mean_cross = group_total(gain * gain_grad) / members
        normed = (values[f].astype(F32).reshape(cells, C) - centre) * inverse
        return inverse * (pre_buf[f] * gain - mean_grad - normed * mean_cross)

    def weight_reduce(q, home, arrivals):
        out = wo.at[q]
        mate = (mate_tm, z)
        mine = core * s.half
        spot = {"y": y, "x": x}
        parts = []
        lo = at = kept = 0
        for p, (first, second, rows) in enumerate(s.parts[q]):
            part = types.SimpleNamespace(p=p, first=first, second=second, lo=lo, at=at, kept=kept)
            part.one = rows // s.size[first]
            part.two = part.one // s.size[second]
            part.r2, part.r3 = arrivals[2 * p], arrivals[2 * p + 1]
            lo, at, kept = lo + rows, at + part.one, kept + part.two
            parts.append(part)

        def span(lo, rows):
            return pl.ds(pl.multiple_of(lo, 16), rows)

        def send(i, src, dst, device):
            pltpu.make_async_remote_copy(
                src_ref=src,
                dst_ref=dst,
                send_sem=w_send.at[q, i],
                recv_sem=w_recv.at[q, i],
                device_id=device,
                device_id_type=MESH,
            ).start()

        def arrived(i, rows):
            bundle(w_recv.at[q, i], wg.at[q, pl.ds(0, rows)])

        def sent(i, rows):
            bundle(w_send.at[q, i], wg.at[q, pl.ds(0, rows)])

        def scatter(i, src, lo, rows, dst, axis):
            for d in range(1, s.size[axis]):
                to = place.rings[axis][d]
                device = (place.lines[axis][d], z)
                send(i, src.at[q, span(lo + to * rows, rows)], dst.at[spot[axis]], device)

        def gather_sum(src, lo, rows, dst, axis):
            total = src[q, span(lo + spot[axis] * rows, rows)].astype(F32)
            for d in range(1, s.size[axis]):
                total += dst[place.rings[axis][d]].astype(F32)
            return total.astype(BF16)

        def step_one():
            arrived(0, 9 * C)
            arrived(1, 5 * C)

            def piece(t, carry):
                rows = span(t * C, C)
                kept = wg[q, span(mine + t * C, C)].astype(F32)
                p1[q, rows] = (kept + r1[q, rows].astype(F32)).astype(BF16)
                return carry

            for part in parts:
                rows = part.one * s.size[part.first]
                lax.fori_loop(part.lo // C, (part.lo + rows) // C, piece, 0)
                scatter(2 + part.p, p1, part.lo, part.one, part.r2, part.first)

        def step_two():
            for part in parts:
                arrived(2 + part.p, (s.size[part.first] - 1) * part.one)
                r1[q, part.at : part.at + part.one] = gather_sum(
                    p1, part.lo, part.one, part.r2, part.first
                )
                scatter(4 + part.p, r1, part.at, part.two, part.r3, part.second)

        def step_three():
            for part in parts:
                arrived(4 + part.p, (s.size[part.second] - 1) * part.two)
                p3[q, part.kept : part.kept + part.two] = gather_sum(
                    r1, part.at, part.two, part.r3, part.second
                )
            spare = s.nz * s.z_rows - s.kept
            if spare:
                p3[q, s.kept :] = jnp.zeros((spare, C), BF16)
            for to in z_ring[1:]:
                send(6, p3.at[q, span(to * s.z_rows, s.z_rows)], r4.at[q, z], (tm, to))

        def step_four():
            arrived(6, (s.nz - 1) * s.z_rows)
            lo = span(z * s.z_rows, s.z_rows)
            total = p3[q, lo].astype(F32)
            for other in z_ring[1:]:
                total += r4[q, other].astype(F32)
            zt[q, lo] = total.astype(BF16)
            for to in z_ring[1:]:
                send(7, zt.at[q, lo], zt.at[q, lo], (tm, to))

        def chunk(part, first, second=None):
            lo = mine + part.lo + first * part.one
            return span(lo, part.one) if second is None else span(lo + second * part.two, part.two)

        def spread(i, rows, axis, each):
            for d in range(1, s.size[axis]):
                device = (place.lines[axis][d], z)
                send(i + (d - 1 if each else 0), out.at[rows], out.at[rows], device)

        def step_five():
            arrived(7, (s.nz - 1) * s.z_rows)
            for part in parts:
                rows = chunk(part, spot[part.first], spot[part.second])
                out[rows] = zt[q, part.kept : part.kept + part.two]
                spread(8 + part.p, rows, part.second, False)

        def deliver(rows):
            send(10, out.at[rows], home.at[rows], mate)

        def step_six():
            for part in parts:
                arrived(8 + part.p, (s.size[part.second] - 1) * part.two)
                rows = chunk(part, spot[part.first])
                spread(11 + 3 * part.p, rows, part.first, True)
            if len(parts) > 1:
                for part in parts:
                    deliver(chunk(part, spot[part.first]))

        def keep():
            return pltpu.make_async_copy(
                out.at[span(mine, s.half)], home.at[span(mine, s.half)], store_sem.at[6 + q]
            )

        def step_seven():
            for d in (1, 3, 2):
                for part in parts:
                    n = s.size[part.first]
                    if d < n:
                        arrived(11 + 3 * part.p + d - 1, part.one)
                        if len(parts) > 1:
                            deliver(chunk(part, place.rings[part.first][n - d]))
            if len(parts) == 1:
                deliver(span(mine, s.half))
            keep().start()

        def step_eight():
            arrived(10, s.half)
            keep().wait()

        def finish():
            sent(0, 9 * C)
            sent(1, 5 * C)
            for part in parts:
                first, second = s.size[part.first], s.size[part.second]
                sent(2 + part.p, (first - 1) * part.one)
                sent(4 + part.p, (second - 1) * part.two)
                sent(8 + part.p, (second - 1) * part.two)
                for d in range(1, first):
                    sent(11 + 3 * part.p + d - 1, part.one)
            sent(6, (s.nz - 1) * s.z_rows)
            sent(7, (s.nz - 1) * s.z_rows)
            sent(10, s.half)

        return [
            None,
            step_one,
            step_two,
            step_three,
            step_four,
            step_five,
            step_six,
            step_seven,
            step_eight,
            finish,
        ]

    def store(i, src, dst):
        copy = pltpu.make_async_copy(src, dst, store_sem.at[i])
        copy.start()
        return copy

    loads[0].wait()
    payload = place.local_stats(place.own(x_ref))
    place.meet()
    place.ar_start(0, 0, payload)
    place.halo_start(0, xe, True)
    loads[1].wait()
    place.halo_start(1, ue, False)
    place.stats_stage(0, 0)
    for load in loads[2:]:
        load.wait()
    gain1, shift1, gain2, shift2 = (vectors[i] for i in range(4))
    place.stats_stage(0, 1)
    place.halo_wait(0, xe)
    copy_first(place, xe)
    place.halo_wait(1, ue)
    blank_next(place, ue)
    stats1 = place.stats_stage(0, 2)

    build_act(xe, a1, stats1, gain1, shift1)
    for f, value in enumerate(conv(a1, w1_ref)):
        he[2 + f, 1 : R + 1] = value.astype(BF16).reshape(R, W, C)
    hidden = place.own_block(he, 2)
    place.ar_start(1, 0, place.local_stats(place.own(hidden)))
    build_grad(ue)
    place.stats_stage(1, 0)
    place.halo_start(2, he, True)
    back_conv(g3, w2_ref)
    place.stats_stage(1, 1)
    place.halo_wait(2, he)
    copy_first(place, he)
    stats2 = place.stats_stage(1, 2)

    second = weight_reduce(1, wo2_hbm, arrivals[4:])
    first = weight_reduce(0, wo1_hbm, arrivals[:4])
    place.ar_start(2, 0, norm_back_sums(hidden, stats2, gain2, shift2))
    build_act(he, a2, stats2, gain2, shift2)
    place.sums_stage(2, 0)
    weight_grad(a2, u_ref, 1)
    place.sums_stage(2, 1)
    second[1]()
    sums2 = place.sums_stage(2, 2)
    for f in range(F):
        value = norm_back_value(hidden, stats2, gain2, sums2, f)
        ge[f, 1 : R + 1] = value.astype(BF16).reshape(R, W, C)
    place.halo_start(3, ge, False)
    weight_grad(a1, place.own_block(ge, 0), 0)
    first[1]()
    second[2]()
    place.halo_wait(3, ge)
    blank_next(place, ge)
    build_grad(ge)
    back_conv(g3, w1_ref)
    place.ar_start(3, 0, norm_back_sums(x_ref, stats1, gain1, shift1))
    first[2]()
    second[3]()
    place.sums_stage(3, 0)
    branch = conv(a2, w2_ref)
    first[3]()
    place.sums_stage(3, 1)
    for f in range(F):
        total = x_ref[f].astype(F32).reshape(cells, C) + branch[f]
        out_ref[f] = total.astype(BF16).reshape(R, W, C)
    stores = [store(0, out_ref, out_hbm)]
    second[4]()
    first[4]()
    sums1 = place.sums_stage(3, 2)
    second[5]()
    first[5]()
    for f in range(F):
        value = norm_back_value(x_ref, stats1, gain1, sums1, f)
        total = u_ref[f].astype(F32).reshape(cells, C) + value
        ig_ref[f] = total.astype(BF16).reshape(R, W, C)
    stores.append(store(1, ig_ref, ig_hbm))
    second[6]()
    first[6]()
    for i, (row, result) in enumerate(zip(sums1 + sums2, (gg1_hbm, sg1_hbm, gg2_hbm, sg2_hbm))):
        results[i] = row
        stores.append(store(2 + i, results.at[i], result))
    second[7]()
    first[7]()
    second[8]()
    first[8]()

    for copy in stores:
        copy.wait()
    second[9]()
    first[9]()
    for k in range(4):
        place.ar_sent(k)
    for q, ref in enumerate((xe, ue, he, ge)):
        place.halo_sent(q, ref)


def finish_kernel(*refs):
    sources, places, (fields, vectors, narrow, wide, load_sem, sem) = refs[:8], refs[8:16], refs[16:]
    copies = []

    def load(i, src, dst):
        copy = pltpu.make_async_copy(src, dst, load_sem.at[i])
        copy.start()
        return copy

    def write(src, dst):
        copy = pltpu.make_async_copy(src, dst, sem.at[len(copies)])
        copy.start()
        copies.append(copy)

    spans = ((0, 9), (9, 10), (19, 9))
    weights = []
    for j, (lo, count) in enumerate(spans):
        for q in range(2):
            rows = pl.ds(lo * C, count * C)
            weights.append(load(2 * j + q, sources[2 + q].at[rows], narrow.at[q, rows]))
    bounce = [(i, fields.at[i]) for i in range(2)] + [(4 + i, vectors.at[i]) for i in range(4)]
    others = [load(6 + n, sources[i], ref) for n, (i, ref) in enumerate(bounce)]
    for j, (lo, count) in enumerate(spans):
        for q in range(2):
            weights[2 * j + q].wait()
            for i in range(3):
                to = (9 * i + 3 * j) * C
                for k in range(3):
                    at = 3 * i + k
                    tap = lo + at + (1 if count == 10 and at >= 5 else 0)
                    block = narrow[q, tap * C : (tap + 1) * C]
                    wide[q, to + k * C : to + (k + 1) * C] = block.astype(F32)
                rows = pl.ds(to, 3 * C)
                write(wide.at[q, rows], places[2 + q].at[rows])
        if j == 0:
            for copy, (i, ref) in zip(others, bounce):
                copy.wait()
                write(ref, places[i])
    for copy in copies:
        copy.wait()


def body(inputs, gain1, shift1, weight1, gain2, shift2, weight2, upstream):
    F, R, W, _ = inputs.shape
    s = plan_of(lax.axis_size("tm"), lax.axis_size("height"), F, R, W)
    E, RE = F + 2, R + 2
    cells = R * W
    hbm = pl.BlockSpec(memory_space=pltpu.HBM)
    field = jax.ShapeDtypeStruct(inputs.shape, BF16)
    weights = jax.ShapeDtypeStruct((s.taps * C, C), BF16)
    vector = jax.ShapeDtypeStruct((1, C), F32)
    wide = pltpu.VMEM((E, RE, W, C), BF16)
    wider = pltpu.VMEM((E, RE, W, 3 * C), BF16)
    arrivals = []
    for parts in s.parts:
        for first, second, rows in parts:
            one = rows // s.size[first]
            arrivals.append(pltpu.VMEM((s.size[first], one, C), BF16))
            arrivals.append(pltpu.VMEM((s.size[second], one // s.size[second], C), BF16))
    room = 60 * 1024 * 1024
    results = pl.pallas_call(
        functools.partial(kernel, s),
        out_shape=[field, field, weights, weights, vector, vector, vector, vector],
        in_specs=[hbm] * 8,
        out_specs=[hbm] * 8,
        scratch_shapes=[
            pltpu.VMEM((27, C, C), BF16),
            pltpu.VMEM((27, C, C), BF16),
            pltpu.VMEM((4, 1, C), F32),
            pltpu.VMEM((F, R, W, C), BF16),
            pltpu.VMEM((F, R, W, C), BF16),
            pltpu.VMEM((2, s.taps * C, C), BF16),
            pltpu.VMEM((4, 1, C), F32),
            wide,
            wide,
            wide,
            wide,
            wider,
            wider,
            wider,
            pltpu.VMEM((F, cells, C), F32),
            pltpu.VMEM((F, cells, C), F32),
            pltpu.VMEM((12, max(s.stages), 2, C), F32),
            pltpu.VMEM((2, s.taps * C, C), BF16),
            pltpu.VMEM((2, s.half, C), BF16),
            pltpu.VMEM((2, s.half, C), BF16),
            pltpu.VMEM((2, s.nz * s.z_rows, C), BF16),
            pltpu.VMEM((2, s.nz, s.z_rows, C), BF16),
            pltpu.VMEM((2, s.nz * s.z_rows, C), BF16),
            arrivals,
            pltpu.SemaphoreType.DMA((12,)),
            pltpu.SemaphoreType.DMA((12,)),
            pltpu.SemaphoreType.DMA((4,)),
            pltpu.SemaphoreType.DMA((4,)),
            pltpu.SemaphoreType.DMA((2, 17)),
            pltpu.SemaphoreType.DMA((2, 17)),
            pltpu.SemaphoreType.DMA((8,)),
            pltpu.SemaphoreType.DMA((8,)),
        ],
        compiler_params=pltpu.CompilerParams(
            collective_id=0, has_side_effects=True, vmem_limit_bytes=room
        ),
        cost_estimate=pl.CostEstimate(
            flops=6 * 2 * F * cells * 27 * C * C, bytes_accessed=8_000_000, transcendentals=1_000_000
        ),
    )(
        inputs,
        upstream,
        weight1.reshape(27, C, C),
        weight2.reshape(27, C, C),
        gain1.reshape(1, C),
        shift1.reshape(1, C),
        gain2.reshape(1, C),
        shift2.reshape(1, C),
    )
    total = jax.ShapeDtypeStruct((27 * C, C), F32)
    output, input_grad, first, second, gg1, sg1, gg2, sg2 = pl.pallas_call(
        finish_kernel,
        out_shape=[field, field, total, total, vector, vector, vector, vector],
        in_specs=[hbm] * 8,
        out_specs=[hbm] * 8,
        scratch_shapes=[
            pltpu.VMEM((2, F, R, W, C), BF16),
            pltpu.VMEM((4, 1, C), F32),
            pltpu.VMEM((2, s.taps * C, C), BF16),
            pltpu.VMEM((2, 27 * C, C), F32),
            pltpu.SemaphoreType.DMA((12,)),
            pltpu.SemaphoreType.DMA((24,)),
        ],
        compiler_params=pltpu.CompilerParams(vmem_limit_bytes=room),
        cost_estimate=pl.CostEstimate(flops=0, bytes_accessed=6_000_000, transcendentals=0),
    )(*results)
    return (
        output,
        input_grad,
        first.reshape(3, 3, 3, C, C),
        second.reshape(3, 3, 3, C, C),
        gg1.reshape(C),
        sg1.reshape(C),
        gg2.reshape(C),
        sg2.reshape(C),
    )


def solution(mesh):
    fields = P("tm", "height", None, None)
    return jax.shard_map(
        body,
        mesh=mesh,
        in_specs=(fields, P(), P(), P(), P(), P(), P(), fields),
        out_specs=(fields, fields, P(), P(), P(), P(), P(), P()),
        check_vma=False,
    )
```

time: 842 us -> 85.1 us (0.10)
  blocking collectives: 458 us -> 0 us
  waiting for transfers between devices: 258 us -> 0 us
  Pallas kernels: 0 us -> 84.3 us
  starting transfers between devices: 32.2 us -> 0 us
  local copies, waits for them, and re-layouts: 29.4 us -> 0 us
  matrix products: 23.7 us -> 0 us
  other arithmetic: 22.3 us -> 0 us
  between operations: 16.4 us -> 0.64 us
    psum x6 -> x0, blocking collectives: 458 us -> none  [the longest x2 160 us: norm_stats(): lax.psum(group_sum(jnp.sum(values, axis=(0, 1, 2))), ('tm', 'height'))]
    psum x1 -> x0, waiting for transfers between devices: 257 us -> none  [body(): lax.psum((first_local, second_local), ('tm', 'height'))]
    pallas_call x0 -> x2, Pallas kernels: none -> 84.3 us  [the longest x1 81 us: body(): pl.pallas_call(functools.partial(kernel, s), out_shape=[field, field, wei...]
    ppermute x12 -> x0, starting transfers between devices: 32.2 us -> none  [the longest x4 16.3 us: extended_2(): lax.ppermute(tail, axis, [(i, (i + 1) % count) for i in range(ends)])]
    dot_general x54 -> x0, matrix products: 23.7 us -> none  [the longest x36 14.4 us: sweep(): jnp.dot(patches, weight[time_tap, row_tap].reshape(-1, channels), preferr...]
    slice x15 -> x0, local copies, waits for them, and re-layouts: 13.4 us -> none  [the longest x10 7.74 us: tap_rows(): extended[:, :, column_tap:column_tap + width_cells]]
    unnamed x245 -> x0, local copies, waits for them, and re-layouts: 12.5 us -> none
    concatenate x30 -> x0, other arithmetic: 9.98 us -> none  [the longest x22 9.21 us: tap_rows(): jnp.concatenate(pieces, axis=-1)]
  transfers between devices with their start and end apart: 13 -> 0, of which waited for: 3 -> 0; matrix products, arithmetic and copies ran while one was open for 4% -> 0% of each run, Pallas kernels for 0% -> 0%
where the time goes in v1:
time: 85.1 us; the launch traced here: 84.9 us
  Pallas kernels  84.3 us (99%)
    pallas_call x1, Pallas kernels, body(): pl.pallas_call(functools.partial(kernel, s), out_shape=[field, field, wei...  81 us
    pallas_call x1, Pallas kernels, body(): pl.pallas_call(finish_kernel, out_shape=[field, field, total, total, vect...  3.26 us

profile of v1, /device:TPU:1, one launch (start us, length us, event | category | flops | bytes accessed | tf_op | source)
XLA Modules:
  0.0 84.9 jit_solution(12421178941290887422)
XLA Ops:
  0.6 81.0 %shard_map.143 = (bf16[2,4,64,128]{3,2,1,0:T(8,128)(2,1)}, bf16[2,4,64,128]{3,2,1,0:T(8,128)(2,1)}, bf16[3584,128]{1,0:T(8,128)(2,1)}, bf16[3584,128]{1,0:T(8,12...) custom-call(bf16[2,4,64,128]{3,2,1,0:T(8,128)(2,1)} %x_hbm.1, ...), custom_call_target="tpu_custom_call" | custom-call | flops 2717908992 | bytes 8000000 | tf_op jit(solution)/shard_map/pallas_call | solution.py:754
  81.7 3.3 %shard_map.144 = (bf16[2,4,64,128]{3,2,1,0:T(8,128)(2,1)}, bf16[2,4,64,128]{3,2,1,0:T(8,128)(2,1)}, f32[3456,128]{1,0:T(8,128)}, f32[3456,128]{1,0:T(8,128)}, f3...) custom-call(bf16[2,4,64,128]{3,2,1,0:T(8,128)(2,1)} %get-tuple-element.24.refs_0_, ...), custom_call_target="tpu_custom_call" | custom-call | bytes 6000000 | tf_op jit(solution)/shard_map/pallas_call | solution.py:810

commit v2 on v1

--- a/solution.py
+++ b/solution.py
@@ -24,10 +24,10 @@
     s.nx = 4 if s.nyx >= 16 else 2
     s.ny = s.nyx // s.nx
     s.frames, s.rows, s.columns = frames, rows, columns
-    s.stages = (s.nz, 2 * s.nx, s.ny)
+    s.stages = (2 * s.nz, s.nyx)
     s.taps = 28
     s.half = s.taps * C // 2
-    s.parts = ((("y", "x", 1024), ("x", "y", s.half - 1024)), (("x", "y", s.half),))
+    s.parts = ((("x", "y", 1024), ("y", "x", s.half - 1024)), (("y", "x", s.half),))
     s.size = {"y": s.ny, "x": s.nx}
     s.kept = s.half // s.nyx
     s.z_rows = 16 * -(-s.kept // 16 // s.nz)
@@ -73,10 +73,8 @@
         self.column = [self.tm_of(q, self.x, core) for q in self.y_ring]
         self.lines = {"y": self.column, "x": self.row}
         self.groups = (
-            (z, [(tm, q) for q in z_ring[1:]]),
-            (self.x * 2 + core, [(mate_tm, z)] + [(q, z) for q in self.row[1:]]
-             + [(q + 1 - 2 * core, z) for q in self.row[1:]]),
-            (self.y, [(q, z) for q in self.column[1:]]),
+            (core * s.nz + z, [(tm, q) for q in z_ring[1:]] + [(mate_tm, q) for q in z_ring]),
+            (yx, [(wrap(yx + d, s.nyx) * 2 + core, z) for d in range(1, s.nyx)]),
         )
         self.tm_next, self.tm_prev = wrap(tm + 1, s.tm), wrap(tm + s.tm - 1, s.tm)
         self.z_next, self.z_prev = z_ring[1], z_ring[-1]
@@ -107,7 +105,7 @@
         self.halo_send, self.halo_recv = halo_send, halo_recv
 
     def ar_start(self, k, stage, payload):
-        i = 3 * k + stage
+        i = 2 * k + stage
         slot, peers = self.groups[stage]
         self.ar[i, slot, 0:1] = payload[0]
         self.ar[i, slot, 1:2] = payload[1]
@@ -122,7 +120,7 @@
             ).start()
 
     def ar_wait(self, k, stage):
-        i = 3 * k + stage
+        i = 2 * k + stage
         n = self.s.stages[stage]
         bundle(self.ar_recv.at[i], self.ar.at[i, pl.ds(0, n - 1)])
         parts = [self.ar[i, j] for j in range(n)]
@@ -130,7 +128,7 @@
 
     def ar_sent(self, k):
         for stage, n in enumerate(self.s.stages):
-            i = 3 * k + stage
+            i = 2 * k + stage
             bundle(self.ar_send.at[i], self.ar.at[i, pl.ds(0, n - 1)])
 
     def local_count(self):
@@ -152,7 +150,7 @@
         for n in self.s.stages[:stage]:
             count = count * n
         joined = self.join_stats(self.ar_wait(k, stage), count)
-        if stage < 2:
+        if stage < 1:
             return self.ar_start(k, stage + 1, joined)
         centre, spread = joined
         return centre, lax.rsqrt(spread / (count * self.s.stages[stage]) + EPSILON)
@@ -160,7 +158,7 @@
     def sums_stage(self, k, stage):
         first, second = self.ar_wait(k, stage)
         totals = sum(first), sum(second)
-        return totals if stage == 2 else self.ar_start(k, stage + 1, totals)
+        return totals if stage == 1 else self.ar_start(k, stage + 1, totals)
 
     def halo_start(self, q, ref, ahead):
         F, R, z = self.s.frames, self.s.rows, self.z
@@ -232,6 +230,8 @@
     sg2_hbm,
     w1_ref,
     w2_ref,
+    wf1,
+    wf2,
     vectors,
     out_ref,
     ig_ref,
@@ -329,14 +329,14 @@
     def dot(a, b):
         return jnp.dot(a, b, preferred_element_type=F32)
 
-    def dot_lanes(a, b):
-        return lax.dot_general(a, b, (((1,), (1,)), ((), ())), preferred_element_type=F32)
+    def turn(src, dst):
+        for at in range(27):
+            dst[at // 9, (at % 9) * C : (at % 9 + 1) * C, :] = src[26 - at].T
 
     def patches(src, f):
         return jnp.concatenate([src[f, j : j + R].reshape(cells, 3 * C) for j in range(3)], axis=1)
 
-    def conv(src, weight):
-        taps = [weight[9 * i : 9 * i + 9].reshape(9 * C, C) for i in range(3)]
+    def conv(src, taps):
         first = dot(patches(src, 0), taps[0])
         second = None
         for f in (1, 2):
@@ -345,26 +345,17 @@
             second = both[:, C:] if second is None else second + both[:, C:]
         return first, second + dot(patches(src, 3), taps[2])
 
+    def taps_of(weight):
+        return [weight[9 * i : 9 * i + 9].reshape(9 * C, C) for i in range(3)]
+
     def back_conv(src, weight):
-        def flipped(i):
-            return jnp.concatenate([weight[9 * i + 8 - jk] for jk in range(9)], axis=1)
-
-        def pair(i):
-            return jnp.concatenate([flipped(i), flipped(i + 1)], axis=0)
-
-        first = dot_lanes(patches(src, 0), flipped(2))
-        second = None
-        for f in (1, 2):
-            both = dot_lanes(patches(src, f), pair(2 - f))
-            first = first + both[:, :C]
-            second = both[:, C:] if second is None else second + both[:, C:]
-        dact[0] = first
-        dact[1] = second + dot_lanes(patches(src, 3), flipped(0))
-
+        dact[0], dact[1] = conv(src, [weight[i] for i in range(3)])
+
+    def back_first(src, weight):
         @pl.when(tm == 0)
         def _():
-            both = dot_lanes(patches(src, 0), pair(0))
-            dact[0] += both[:, :C] + both[:, C:] + dot_lanes(patches(src, 1), flipped(0))
+            both = dot(patches(src, 0), jnp.concatenate([weight[1], weight[2]], axis=1))
+            dact[0] += both[:, :C] + both[:, C:] + dot(patches(src, 1), weight[2])
 
     def weight_grad(act, grad, q):
         turned = [grad[f].reshape(cells, C).T for f in range(F)]
@@ -521,17 +512,17 @@
             lo = mine + part.lo + first * part.one
             return span(lo, part.one) if second is None else span(lo + second * part.two, part.two)
 
-        def spread(i, rows, axis, each):
+        def spread(i, rows, axis):
             for d in range(1, s.size[axis]):
                 device = (place.lines[axis][d], z)
-                send(i + (d - 1 if each else 0), out.at[rows], out.at[rows], device)
+                send(i, out.at[rows], out.at[rows], device)
 
         def step_five():
             arrived(7, (s.nz - 1) * s.z_rows)
             for part in parts:
                 rows = chunk(part, spot[part.first], spot[part.second])
                 out[rows] = zt[q, part.kept : part.kept + part.two]
-                spread(8 + part.p, rows, part.second, False)
+                spread(8 + part.p, rows, part.second)
 
         def deliver(rows):
             send(10, out.at[rows], home.at[rows], mate)
@@ -540,10 +531,7 @@
             for part in parts:
                 arrived(8 + part.p, (s.size[part.second] - 1) * part.two)
                 rows = chunk(part, spot[part.first])
-                spread(11 + 3 * part.p, rows, part.first, True)
-            if len(parts) > 1:
-                for part in parts:
-                    deliver(chunk(part, spot[part.first]))
+                spread(11 + part.p, rows, part.first)
 
         def keep():
             return pltpu.make_async_copy(
@@ -551,15 +539,9 @@
             )
 
         def step_seven():
-            for d in (1, 3, 2):
-                for part in parts:
-                    n = s.size[part.first]
-                    if d < n:
-                        arrived(11 + 3 * part.p + d - 1, part.one)
-                        if len(parts) > 1:
-                            deliver(chunk(part, place.rings[part.first][n - d]))
-            if len(parts) == 1:
-                deliver(span(mine, s.half))
+            for part in parts:
+                arrived(11 + part.p, (s.size[part.first] - 1) * part.one)
+                deliver(span(mine + part.lo, part.one * s.size[part.first]))
             keep().start()
 
         def step_eight():
@@ -574,8 +556,7 @@
                 sent(2 + part.p, (first - 1) * part.one)
                 sent(4 + part.p, (second - 1) * part.two)
                 sent(8 + part.p, (second - 1) * part.two)
-                for d in range(1, first):
-                    sent(11 + 3 * part.p + d - 1, part.one)
+                sent(11 + part.p, (first - 1) * part.one)
             sent(6, (s.nz - 1) * s.z_rows)
             sent(7, (s.nz - 1) * s.z_rows)
             sent(10, s.half)
@@ -593,6 +574,190 @@
             finish,
         ]
 
+    def weight_relay(q, home, arrivals):
+        out = wo.at[q]
+        mate = (mate_tm, z)
+        mine = core * s.half
+        spot = {"y": y, "x": x}
+        parts = []
+        lo = at = kept = 0
+        for p, (first, second, rows) in enumerate(s.parts[q]):
+            part = types.SimpleNamespace(p=p, first=first, second=second, lo=lo, at=at, kept=kept)
+            part.one = rows // s.size[first]
+            part.two = part.one // s.size[second]
+            part.ra, part.rb, part.r3 = arrivals[3 * p : 3 * p + 3]
+            part.me, part.ahead, part.far, part.behind = place.rings[first]
+            line = place.lines[first]
+            part.to_ahead, part.to_behind = (line[1], z), (line[3], z)
+            lo, at, kept = lo + rows, at + part.one, kept + part.two
+            parts.append(part)
+
+        def span(lo, rows):
+            return pl.ds(pl.multiple_of(lo, 16), rows)
+
+        def send(i, src, dst, device):
+            pltpu.make_async_remote_copy(
+                src_ref=src,
+                dst_ref=dst,
+                send_sem=w_send.at[q, i],
+                recv_sem=w_recv.at[q, i],
+                device_id=device,
+                device_id_type=MESH,
+            ).start()
+
+        def arrived(i, rows):
+            bundle(w_recv.at[q, i], wg.at[q, pl.ds(0, rows)])
+
+        def sent(i, rows):
+            bundle(w_send.at[q, i], wg.at[q, pl.ds(0, rows)])
+
+        def scatter(i, src, lo, rows, dst, axis):
+            for d in range(1, s.size[axis]):
+                to = place.rings[axis][d]
+                device = (place.lines[axis][d], z)
+                send(i, src.at[q, span(lo + to * rows, rows)], dst.at[spot[axis]], device)
+
+        def gather_sum(src, lo, rows, dst, axis):
+            total = src[q, span(lo + spot[axis] * rows, rows)].astype(F32)
+            for d in range(1, s.size[axis]):
+                total += dst[place.rings[axis][d]].astype(F32)
+            return total.astype(BF16)
+
+        def step_one():
+            arrived(0, 9 * C)
+            arrived(1, 5 * C)
+
+            def piece(t, carry):
+                rows = span(t * C, C)
+                kept = wg[q, span(mine + t * C, C)].astype(F32)
+                p1[q, rows] = (kept + r1[q, rows].astype(F32)).astype(BF16)
+                return carry
+
+            for part in parts:
+                lax.fori_loop(part.lo // C, (part.lo + 4 * part.one) // C, piece, 0)
+                half = part.one // 2
+                lo = part.lo + part.far * part.one
+                send(2 + part.p, p1.at[q, span(lo, half)], part.ra.at[0], part.to_ahead)
+                send(2 + part.p, p1.at[q, span(lo + half, half)], part.ra.at[1], part.to_behind)
+
+        def step_two():
+            for part in parts:
+                half = part.one // 2
+                arrived(2 + part.p, part.one)
+                for side, to, skip in ((0, part.ahead, 0), (1, part.behind, half)):
+                    rows = span(part.lo + to * part.one + skip, half)
+                    total = p1[q, rows].astype(F32) + part.ra[side].astype(F32)
+                    p1[q, rows] = total.astype(BF16)
+                for side, to, device in (
+                    (0, part.ahead, part.to_ahead),
+                    (1, part.behind, part.to_behind),
+                ):
+                    rows = span(part.lo + to * part.one, part.one)
+                    send(4 + part.p, p1.at[q, rows], part.rb.at[side], device)
+
+        def step_three():
+            for part in parts:
+                arrived(4 + part.p, 2 * part.one)
+                total = p1[q, span(part.lo + part.me * part.one, part.one)].astype(F32)
+                total += part.rb[0].astype(F32) + part.rb[1].astype(F32)
+                r1[q, part.at : part.at + part.one] = total.astype(BF16)
+                scatter(6 + part.p, r1, part.at, part.two, part.r3, part.second)
+
+        def step_reduced():
+            for part in parts:
+                arrived(6 + part.p, (s.size[part.second] - 1) * part.two)
+                p3[q, part.kept : part.kept + part.two] = gather_sum(
+                    r1, part.at, part.two, part.r3, part.second
+                )
+            spare = s.nz * s.z_rows - s.kept
+            if spare:
+                p3[q, s.kept :] = jnp.zeros((spare, C), BF16)
+            for to in z_ring[1:]:
+                send(8, p3.at[q, span(to * s.z_rows, s.z_rows)], r4.at[q, z], (tm, to))
+
+        def step_four():
+            arrived(8, (s.nz - 1) * s.z_rows)
+            lo = span(z * s.z_rows, s.z_rows)
+            total = p3[q, lo].astype(F32)
+            for other in z_ring[1:]:
+                total += r4[q, other].astype(F32)
+            zt[q, lo] = total.astype(BF16)
+            for to in z_ring[1:]:
+                send(9, zt.at[q, lo], zt.at[q, lo], (tm, to))
+
+        def chunk(part, first, skip=0, rows=None):
+            return span(mine + part.lo + first * part.one + skip, part.one if rows is None else rows)
+
+        def step_five():
+            arrived(9, (s.nz - 1) * s.z_rows)
+            for part in parts:
+                rows = chunk(part, part.me, spot[part.second] * part.two, part.two)
+                out[rows] = zt[q, part.kept : part.kept + part.two]
+                for d in range(1, s.size[part.second]):
+                    device = (place.lines[part.second][d], z)
+                    send(10 + part.p, out.at[rows], out.at[rows], device)
+
+        def deliver(rows):
+            send(16, out.at[rows], home.at[rows], mate)
+
+        def step_six():
+            for part in parts:
+                arrived(10 + part.p, (s.size[part.second] - 1) * part.two)
+                rows = chunk(part, part.me)
+                send(12 + part.p, out.at[rows], out.at[rows], part.to_ahead)
+                send(12 + part.p, out.at[rows], out.at[rows], part.to_behind)
+        def step_seven():
+            for part in parts:
+                half = part.one // 2
+                arrived(12 + part.p, 2 * part.one)
+                rows = chunk(part, part.behind, 0, half)
+                send(14 + part.p, out.at[rows], out.at[rows], part.to_ahead)
+                rows = chunk(part, part.ahead, half, half)
+                send(14 + part.p, out.at[rows], out.at[rows], part.to_behind)
+        def keep():
+            return pltpu.make_async_copy(
+                out.at[span(mine, s.half)], home.at[span(mine, s.half)], store_sem.at[6 + q]
+            )
+
+        def step_eight():
+            for part in parts:
+                arrived(14 + part.p, part.one)
+            deliver(span(mine, s.half))
+            keep().start()
+
+        def step_nine():
+            arrived(16, s.half)
+            keep().wait()
+
+        def finish():
+            sent(0, 9 * C)
+            sent(1, 5 * C)
+            for part in parts:
+                sent(2 + part.p, part.one)
+                sent(4 + part.p, 2 * part.one)
+                sent(6 + part.p, (s.size[part.second] - 1) * part.two)
+                sent(10 + part.p, (s.size[part.second] - 1) * part.two)
+                sent(12 + part.p, 2 * part.one)
+                sent(14 + part.p, part.one)
+            sent(8, (s.nz - 1) * s.z_rows)
+            sent(9, (s.nz - 1) * s.z_rows)
+            sent(16, s.half)
+
+        return [
+            None,
+            step_one,
+            step_two,
+            step_three,
+            step_reduced,
+            step_four,
+            step_five,
+            step_six,
+            step_seven,
+            step_eight,
+            step_nine,
+            finish,
+        ]
+
     def store(i, src, dst):
         copy = pltpu.make_async_copy(src, dst, store_sem.at[i])
         copy.start()
@@ -605,85 +770,87 @@
     place.halo_start(0, xe, True)
     loads[1].wait()
     place.halo_start(1, ue, False)
-    place.stats_stage(0, 0)
     for load in loads[2:]:
         load.wait()
     gain1, shift1, gain2, shift2 = (vectors[i] for i in range(4))
-    place.stats_stage(0, 1)
+    turn(w2_ref, wf2)
+    place.stats_stage(0, 0)
+    turn(w1_ref, wf1)
     place.halo_wait(0, xe)
     copy_first(place, xe)
-    place.halo_wait(1, ue)
-    blank_next(place, ue)
-    stats1 = place.stats_stage(0, 2)
+    stats1 = place.stats_stage(0, 1)
 
     build_act(xe, a1, stats1, gain1, shift1)
-    for f, value in enumerate(conv(a1, w1_ref)):
+    for f, value in enumerate(conv(a1, taps_of(w1_ref))):
         he[2 + f, 1 : R + 1] = value.astype(BF16).reshape(R, W, C)
     hidden = place.own_block(he, 2)
     place.ar_start(1, 0, place.local_stats(place.own(hidden)))
+    place.halo_wait(1, ue)
+    blank_next(place, ue)
     build_grad(ue)
     place.stats_stage(1, 0)
     place.halo_start(2, he, True)
-    back_conv(g3, w2_ref)
-    place.stats_stage(1, 1)
+    back_conv(g3, wf2)
+    back_first(g3, wf2)
     place.halo_wait(2, he)
     copy_first(place, he)
-    stats2 = place.stats_stage(1, 2)
-
-    second = weight_reduce(1, wo2_hbm, arrivals[4:])
+    stats2 = place.stats_stage(1, 1)
+
+    second = weight_relay(1, wo2_hbm, arrivals[4:])
     first = weight_reduce(0, wo1_hbm, arrivals[:4])
     place.ar_start(2, 0, norm_back_sums(hidden, stats2, gain2, shift2))
     build_act(he, a2, stats2, gain2, shift2)
     place.sums_stage(2, 0)
     weight_grad(a2, u_ref, 1)
-    place.sums_stage(2, 1)
-    second[1]()
-    sums2 = place.sums_stage(2, 2)
+    sums2 = place.sums_stage(2, 1)
     for f in range(F):
         value = norm_back_value(hidden, stats2, gain2, sums2, f)
         ge[f, 1 : R + 1] = value.astype(BF16).reshape(R, W, C)
     place.halo_start(3, ge, False)
+    second[1]()
     weight_grad(a1, place.own_block(ge, 0), 0)
+    second[2]()
     first[1]()
-    second[2]()
     place.halo_wait(3, ge)
     blank_next(place, ge)
     build_grad(ge)
-    back_conv(g3, w1_ref)
+    second[3]()
+    back_conv(g3, wf1)
+    back_first(g3, wf1)
     place.ar_start(3, 0, norm_back_sums(x_ref, stats1, gain1, shift1))
     first[2]()
-    second[3]()
-    place.sums_stage(3, 0)
-    branch = conv(a2, w2_ref)
-    first[3]()
-    place.sums_stage(3, 1)
+    second[4]()
+    branch = conv(a2, taps_of(w2_ref))
     for f in range(F):
         total = x_ref[f].astype(F32).reshape(cells, C) + branch[f]
         out_ref[f] = total.astype(BF16).reshape(R, W, C)
     stores = [store(0, out_ref, out_hbm)]
-    second[4]()
+    first[3]()
+    place.sums_stage(3, 0)
+    second[5]()
     first[4]()
-    sums1 = place.sums_stage(3, 2)
-    second[5]()
+    second[6]()
+    sums1 = place.sums_stage(3, 1)
     first[5]()
+    second[7]()
     for f in range(F):
         value = norm_back_value(x_ref, stats1, gain1, sums1, f)
         total = u_ref[f].astype(F32).reshape(cells, C) + value
         ig_ref[f] = total.astype(BF16).reshape(R, W, C)
     stores.append(store(1, ig_ref, ig_hbm))
-    second[6]()
     first[6]()
+    second[8]()
     for i, (row, result) in enumerate(zip(sums1 + sums2, (gg1_hbm, sg1_hbm, gg2_hbm, sg2_hbm))):
         results[i] = row
         stores.append(store(2 + i, results.at[i], result))
-    second[7]()
+    second[9]()
     first[7]()
-    second[8]()
+    second[10]()
     first[8]()
 
     for copy in stores:
         copy.wait()
-    second[9]()
+    second[11]()
     first[9]()
     for k in range(4):
         place.ar_sent(k)
@@ -745,11 +912,15 @@
     wide = pltpu.VMEM((E, RE, W, C), BF16)
     wider = pltpu.VMEM((E, RE, W, 3 * C), BF16)
     arrivals = []
-    for parts in s.parts:
-        for first, second, rows in parts:
-            one = rows // s.size[first]
-            arrivals.append(pltpu.VMEM((s.size[first], one, C), BF16))
-            arrivals.append(pltpu.VMEM((s.size[second], one // s.size[second], C), BF16))
+    for first, second, rows in s.parts[0]:
+        one = rows // s.size[first]
+        arrivals.append(pltpu.VMEM((s.size[first], one, C), BF16))
+        arrivals.append(pltpu.VMEM((s.size[second], one // s.size[second], C), BF16))
+    for first, second, rows in s.parts[1]:
+        one = rows // s.size[first]
+        arrivals.append(pltpu.VMEM((2, one // 2, C), BF16))
+        arrivals.append(pltpu.VMEM((2, one, C), BF16))
+        arrivals.append(pltpu.VMEM((s.size[second], one // s.size[second], C), BF16))
     room = 60 * 1024 * 1024
     results = pl.pallas_call(
         functools.partial(kernel, s),
@@ -759,6 +930,8 @@
         scratch_shapes=[
             pltpu.VMEM((27, C, C), BF16),
             pltpu.VMEM((27, C, C), BF16),
+            pltpu.VMEM((3, 9 * C, C), BF16),
+            pltpu.VMEM((3, 9 * C, C), BF16),
             pltpu.VMEM((4, 1, C), F32),
             pltpu.VMEM((F, R, W, C), BF16),
             pltpu.VMEM((F, R, W, C), BF16),
@@ -773,7 +946,7 @@
             wider,
             pltpu.VMEM((F, cells, C), F32),
             pltpu.VMEM((F, cells, C), F32),
-            pltpu.VMEM((12, max(s.stages), 2, C), F32),
+            pltpu.VMEM((8, max(s.stages), 2, C), F32),
             pltpu.VMEM((2, s.taps * C, C), BF16),
             pltpu.VMEM((2, s.half, C), BF16),
             pltpu.VMEM((2, s.half, C), BF16),
@@ -781,8 +954,8 @@
             pltpu.VMEM((2, s.nz, s.z_rows, C), BF16),
             pltpu.VMEM((2, s.nz * s.z_rows, C), BF16),
             arrivals,
-            pltpu.SemaphoreType.DMA((12,)),
-            pltpu.SemaphoreType.DMA((12,)),
+            pltpu.SemaphoreType.DMA((8,)),
+            pltpu.SemaphoreType.DMA((8,)),
             pltpu.SemaphoreType.DMA((4,)),
             pltpu.SemaphoreType.DMA((4,)),
             pltpu.SemaphoreType.DMA((2, 17)),

time: 85.1 us -> 84.8 us (level)
  no operation moved by 1% of the time
where the time goes in v2:
time: 84.8 us; the launch traced here: 84.6 us
  Pallas kernels  84 us (99%)
    pallas_call x1, Pallas kernels, body(): pl.pallas_call(functools.partial(kernel, s), out_shape=[field, field, wei...  80.7 us
    pallas_call x1, Pallas kernels, body(): pl.pallas_call(finish_kernel, out_shape=[field, field, total, total, vect...  3.26 us

profile of v2, /device:TPU:1, one launch (start us, length us, event | category | flops | bytes accessed | tf_op | source)
XLA Modules:
  0.0 84.6 jit_solution(770150211106397674)
XLA Ops:
  0.6 80.7 %shard_map.143 = (bf16[2,4,64,128]{3,2,1,0:T(8,128)(2,1)}, bf16[2,4,64,128]{3,2,1,0:T(8,128)(2,1)}, bf16[3584,128]{1,0:T(8,128)(2,1)}, bf16[3584,128]{1,0:T(8,12...) custom-call(bf16[2,4,64,128]{3,2,1,0:T(8,128)(2,1)} %x_hbm.1, ...), custom_call_target="tpu_custom_call" | custom-call | flops 2717908992 | bytes 8000000 | tf_op jit(solution)/shard_map/pallas_call | solution.py:925
  81.4 3.3 %shard_map.144 = (bf16[2,4,64,128]{3,2,1,0:T(8,128)(2,1)}, bf16[2,4,64,128]{3,2,1,0:T(8,128)(2,1)}, f32[3456,128]{1,0:T(8,128)}, f32[3456,128]{1,0:T(8,128)}, f3...) custom-call(bf16[2,4,64,128]{3,2,1,0:T(8,128)(2,1)} %get-tuple-element.24.refs_0_, ...), custom_call_target="tpu_custom_call" | custom-call | bytes 6000000 | tf_op jit(solution)/shard_map/pallas_call | solution.py:983

commit v3 on v1

--- a/solution.py
+++ b/solution.py
@@ -24,13 +24,20 @@
     s.nx = 4 if s.nyx >= 16 else 2
     s.ny = s.nyx // s.nx
     s.frames, s.rows, s.columns = frames, rows, columns
-    s.stages = (s.nz, 2 * s.nx, s.ny)
+    s.stages = (2 * s.nz, s.nyx)
     s.taps = 28
     s.half = s.taps * C // 2
-    s.parts = ((("y", "x", 1024), ("x", "y", s.half - 1024)), (("x", "y", s.half),))
+    most = min(s.nz - 1, 7) if s.nz > 2 else 2
+    s.parts = (
+        (("x", "y", 1024, 0, s.nz // 2), ("y", "x", s.half - 1024, s.nz // 2, most - s.nz // 2)),
+        (("y", "x", s.half, 0, most),),
+    )
     s.size = {"y": s.ny, "x": s.nx}
-    s.kept = s.half // s.nyx
-    s.z_rows = 16 * -(-s.kept // 16 // s.nz)
+    s.tile = max(
+        rows // s.size[first] // (s.size[second] * count)
+        for parts in s.parts
+        for first, second, rows, _, count in parts
+    )
     return s
 
 
@@ -73,10 +80,8 @@
         self.column = [self.tm_of(q, self.x, core) for q in self.y_ring]
         self.lines = {"y": self.column, "x": self.row}
         self.groups = (
-            (z, [(tm, q) for q in z_ring[1:]]),
-            (self.x * 2 + core, [(mate_tm, z)] + [(q, z) for q in self.row[1:]]
-             + [(q + 1 - 2 * core, z) for q in self.row[1:]]),
-            (self.y, [(q, z) for q in self.column[1:]]),
+            (core * s.nz + z, [(tm, q) for q in z_ring[1:]] + [(mate_tm, q) for q in z_ring]),
+            (yx, [(wrap(yx + d, s.nyx) * 2 + core, z) for d in range(1, s.nyx)]),
         )
         self.tm_next, self.tm_prev = wrap(tm + 1, s.tm), wrap(tm + s.tm - 1, s.tm)
         self.z_next, self.z_prev = z_ring[1], z_ring[-1]
@@ -84,6 +89,9 @@
         self.partners = self.partners + [
             (t, q) for t in (self.tm_next, self.tm_prev) for q in (z, self.z_next, self.z_prev)
         ]
+        self.partners = self.partners + [
+            (t, q) for line in (self.row, self.column) for t in line[1:] for q in z_ring[1:]
+        ]
 
     def tm_of(self, y, x, core):
         return (y * self.s.nx + x) * 2 + core
@@ -107,7 +115,7 @@
         self.halo_send, self.halo_recv = halo_send, halo_recv
 
     def ar_start(self, k, stage, payload):
-        i = 3 * k + stage
+        i = 2 * k + stage
         slot, peers = self.groups[stage]
         self.ar[i, slot, 0:1] = payload[0]
         self.ar[i, slot, 1:2] = payload[1]
@@ -122,7 +130,7 @@
             ).start()
 
     def ar_wait(self, k, stage):
-        i = 3 * k + stage
+        i = 2 * k + stage
         n = self.s.stages[stage]
         bundle(self.ar_recv.at[i], self.ar.at[i, pl.ds(0, n - 1)])
         parts = [self.ar[i, j] for j in range(n)]
@@ -130,7 +138,7 @@
 
     def ar_sent(self, k):
         for stage, n in enumerate(self.s.stages):
-            i = 3 * k + stage
+            i = 2 * k + stage
             bundle(self.ar_send.at[i], self.ar.at[i, pl.ds(0, n - 1)])
 
     def local_count(self):
@@ -152,7 +160,7 @@
         for n in self.s.stages[:stage]:
             count = count * n
         joined = self.join_stats(self.ar_wait(k, stage), count)
-        if stage < 2:
+        if stage < 1:
             return self.ar_start(k, stage + 1, joined)
         centre, spread = joined
         return centre, lax.rsqrt(spread / (count * self.s.stages[stage]) + EPSILON)
@@ -160,7 +168,7 @@
     def sums_stage(self, k, stage):
         first, second = self.ar_wait(k, stage)
         totals = sum(first), sum(second)
-        return totals if stage == 2 else self.ar_start(k, stage + 1, totals)
+        return totals if stage == 1 else self.ar_start(k, stage + 1, totals)
 
     def halo_start(self, q, ref, ahead):
         F, R, z = self.s.frames, self.s.rows, self.z
@@ -232,6 +240,8 @@
     sg2_hbm,
     w1_ref,
     w2_ref,
+    wf1,
+    wf2,
     vectors,
     out_ref,
     ig_ref,
@@ -250,9 +260,7 @@
     wg,
     r1,
     p1,
-    p3,
-    r4,
-    zt,
+    rx,
     arrivals,
     ar_send,
     ar_recv,
@@ -329,14 +337,14 @@
     def dot(a, b):
         return jnp.dot(a, b, preferred_element_type=F32)
 
-    def dot_lanes(a, b):
-        return lax.dot_general(a, b, (((1,), (1,)), ((), ())), preferred_element_type=F32)
+    def turn(src, dst):
+        for at in range(27):
+            dst[at // 9, (at % 9) * C : (at % 9 + 1) * C, :] = src[26 - at].T
 
     def patches(src, f):
         return jnp.concatenate([src[f, j : j + R].reshape(cells, 3 * C) for j in range(3)], axis=1)
 
-    def conv(src, weight):
-        taps = [weight[9 * i : 9 * i + 9].reshape(9 * C, C) for i in range(3)]
+    def conv(src, taps):
         first = dot(patches(src, 0), taps[0])
         second = None
         for f in (1, 2):
@@ -345,26 +353,17 @@
             second = both[:, C:] if second is None else second + both[:, C:]
         return first, second + dot(patches(src, 3), taps[2])
 
+    def taps_of(weight):
+        return [weight[9 * i : 9 * i + 9].reshape(9 * C, C) for i in range(3)]
+
     def back_conv(src, weight):
-        def flipped(i):
-            return jnp.concatenate([weight[9 * i + 8 - jk] for jk in range(9)], axis=1)
-
-        def pair(i):
-            return jnp.concatenate([flipped(i), flipped(i + 1)], axis=0)
-
-        first = dot_lanes(patches(src, 0), flipped(2))
-        second = None
-        for f in (1, 2):
-            both = dot_lanes(patches(src, f), pair(2 - f))
-            first = first + both[:, :C]
-            second = both[:, C:] if second is None else second + both[:, C:]
-        dact[0] = first
-        dact[1] = second + dot_lanes(patches(src, 3), flipped(0))
-
+        dact[0], dact[1] = conv(src, [weight[i] for i in range(3)])
+
+    def back_first(src, weight):
         @pl.when(tm == 0)
         def _():
-            both = dot_lanes(patches(src, 0), pair(0))
-            dact[0] += both[:, :C] + both[:, C:] + dot_lanes(patches(src, 1), flipped(0))
+            both = dot(patches(src, 0), jnp.concatenate([weight[1], weight[2]], axis=1))
+            dact[0] += both[:, :C] + both[:, C:] + dot(patches(src, 1), weight[2])
 
     def weight_grad(act, grad, q):
         turned = [grad[f].reshape(cells, C).T for f in range(F)]
@@ -426,30 +425,36 @@
         normed = (values[f].astype(F32).reshape(cells, C) - centre) * inverse
         return inverse * (pre_buf[f] * gain - mean_grad - normed * mean_cross)
 
-    def weight_reduce(q, home, arrivals):
+    def weight_sum(q, home, arrivals, relay):
         out = wo.at[q]
         mate = (mate_tm, z)
         mine = core * s.half
         spot = {"y": y, "x": x}
         parts = []
-        lo = at = kept = 0
-        for p, (first, second, rows) in enumerate(s.parts[q]):
-            part = types.SimpleNamespace(p=p, first=first, second=second, lo=lo, at=at, kept=kept)
-            part.one = rows // s.size[first]
-            part.two = part.one // s.size[second]
-            part.r2, part.r3 = arrivals[2 * p], arrivals[2 * p + 1]
-            lo, at, kept = lo + rows, at + part.one, kept + part.two
+        lo = at = 0
+        for p, (first, second, rows, z_lo, z_count) in enumerate(s.parts[q]):
+            part = types.SimpleNamespace(p=p, first=first, second=second, lo=lo, at=at, z_lo=z_lo)
+            part.zs = range(z_lo, z_lo + z_count)
+            part.n = s.size[first]
+            part.one = rows // part.n
+            part.tile = part.one // (s.size[second] * z_count)
+            part.ring, part.line = place.rings[first], place.lines[first]
+            part.owner = jnp.logical_and(z >= z_lo, z < z_lo + z_count)
+            part.slot = z * s.size[second] + spot[second]
+            part.own = ((z - z_lo) * s.size[second] + spot[second]) * part.tile
+            lo, at = lo + rows, at + part.one
             parts.append(part)
+        plane = s.nz * 4
 
         def span(lo, rows):
             return pl.ds(pl.multiple_of(lo, 16), rows)
 
-        def send(i, src, dst, device):
+        def send(i, src, dst, device, arrival=None):
             pltpu.make_async_remote_copy(
                 src_ref=src,
                 dst_ref=dst,
                 send_sem=w_send.at[q, i],
-                recv_sem=w_recv.at[q, i],
+                recv_sem=w_recv.at[q, i if arrival is None else arrival],
                 device_id=device,
                 device_id_type=MESH,
             ).start()
@@ -460,138 +465,167 @@
         def sent(i, rows):
             bundle(w_send.at[q, i], wg.at[q, pl.ds(0, rows)])
 
-        def scatter(i, src, lo, rows, dst, axis):
-            for d in range(1, s.size[axis]):
-                to = place.rings[axis][d]
-                device = (place.lines[axis][d], z)
-                send(i, src.at[q, span(lo + to * rows, rows)], dst.at[spot[axis]], device)
-
-        def gather_sum(src, lo, rows, dst, axis):
-            total = src[q, span(lo + spot[axis] * rows, rows)].astype(F32)
-            for d in range(1, s.size[axis]):
-                total += dst[place.rings[axis][d]].astype(F32)
-            return total.astype(BF16)
-
-        def step_one():
-            arrived(0, 9 * C)
-            arrived(1, 5 * C)
-
+        def add_mate(part):
             def piece(t, carry):
                 rows = span(t * C, C)
                 kept = wg[q, span(mine + t * C, C)].astype(F32)
                 p1[q, rows] = (kept + r1[q, rows].astype(F32)).astype(BF16)
                 return carry
 
+            lax.fori_loop(part.lo // C, (part.lo + part.n * part.one) // C, piece, 0)
+
+        def rows_of(part, i, skip=0, rows=None):
+            return span(part.lo + i * part.one + skip, part.one if rows is None else rows)
+
+        def step_mate():
+            arrived(0, 9 * C)
+            arrived(1, 5 * C)
             for part in parts:
-                rows = part.one * s.size[part.first]
-                lax.fori_loop(part.lo // C, (part.lo + rows) // C, piece, 0)
-                scatter(2 + part.p, p1, part.lo, part.one, part.r2, part.first)
-
-        def step_two():
+                add_mate(part)
+                if relay:
+                    half = part.one // 2
+                    far = part.ring[2]
+                    one = p1.at[q, rows_of(part, far, 0, half)]
+                    two = p1.at[q, rows_of(part, far, half, half)]
+                    send(2, one, arrivals[0].at[0], (part.line[1], z))
+                    send(2, two, arrivals[0].at[1], (part.line[3], z))
+                else:
+                    for d in range(1, part.n):
+                        src = p1.at[q, rows_of(part, part.ring[d])]
+                        dst = arrivals[part.p].at[part.ring[0]]
+                        send(2 + part.p, src, dst, (part.line[d], z))
+
+        def step_relay():
+            (part,) = parts
+            half = part.one // 2
+            arrived(2, part.one)
+            for side, to, skip in ((0, 1, 0), (1, 3, half)):
+                rows = rows_of(part, part.ring[to], skip, half)
+                total = p1[q, rows].astype(F32) + arrivals[0][side].astype(F32)
+                p1[q, rows] = total.astype(BF16)
+            for side, to in ((0, 1), (1, 3)):
+                src = p1.at[q, rows_of(part, part.ring[to])]
+                send(3, src, arrivals[1].at[side], (part.line[to], z))
+
+        def step_plane():
             for part in parts:
-                arrived(2 + part.p, (s.size[part.first] - 1) * part.one)
-                r1[q, part.at : part.at + part.one] = gather_sum(
-                    p1, part.lo, part.one, part.r2, part.first
-                )
-                scatter(4 + part.p, r1, part.at, part.two, part.r3, part.second)
-
-        def step_three():
+                total = p1[q, rows_of(part, part.ring[0])].astype(F32)
+                if relay:
+                    arrived(3, 2 * part.one)
+                    total += arrivals[1][0].astype(F32) + arrivals[1][1].astype(F32)
+                else:
+                    arrived(2 + part.p, (part.n - 1) * part.one)
+                    for d in range(1, part.n):
+                        total += arrivals[part.p][part.ring[d]].astype(F32)
+                r1[q, part.at : part.at + part.one] = total.astype(BF16)
+                across, line = place.rings[part.second], place.lines[part.second]
+                for d in range(s.size[part.second]):
+                    for owner_z in part.zs:
+
+                        def go(part=part, d=d, owner_z=owner_z, across=across, line=line):
+                            tile = (owner_z - part.z_lo) * s.size[part.second] + across[d]
+                            src = r1.at[q, span(part.at + tile * part.tile, part.tile)]
+                            dst = rx.at[q, part.slot, pl.ds(0, part.tile)]
+                            send(4 + part.p, src, dst, (line[d], owner_z), 4)
+
+                        if d:
+                            go()
+                        else:
+                            pl.when(z != owner_z)(go)
+
+        def step_own():
             for part in parts:
-                arrived(4 + part.p, (s.size[part.second] - 1) * part.two)
-                p3[q, part.kept : part.kept + part.two] = gather_sum(
-                    r1, part.at, part.two, part.r3, part.second
-                )
-            spare = s.nz * s.z_rows - s.kept
-            if spare:
-                p3[q, s.kept :] = jnp.zeros((spare, C), BF16)
-            for to in z_ring[1:]:
-                send(6, p3.at[q, span(to * s.z_rows, s.z_rows)], r4.at[q, z], (tm, to))
-
-        def step_four():
-            arrived(6, (s.nz - 1) * s.z_rows)
-            lo = span(z * s.z_rows, s.z_rows)
-            total = p3[q, lo].astype(F32)
-            for other in z_ring[1:]:
-                total += r4[q, other].astype(F32)
-            zt[q, lo] = total.astype(BF16)
-            for to in z_ring[1:]:
-                send(7, zt.at[q, lo], zt.at[q, lo], (tm, to))
-
-        def chunk(part, first, second=None):
-            lo = mine + part.lo + first * part.one
-            return span(lo, part.one) if second is None else span(lo + second * part.two, part.two)
-
-        def spread(i, rows, axis, each):
-            for d in range(1, s.size[axis]):
-                device = (place.lines[axis][d], z)
-                send(i + (d - 1 if each else 0), out.at[rows], out.at[rows], device)
-
-        def step_five():
-            arrived(7, (s.nz - 1) * s.z_rows)
+
+                @pl.when(part.owner)
+                def _(part=part):
+                    arrived(4, (plane - 1) * part.tile)
+                    tile = pl.ds(0, part.tile)
+                    rx[q, part.slot, tile] = r1[q, span(part.at + part.own, part.tile)]
+                    total = rx[q, 0, tile].astype(F32)
+                    for j in range(1, plane):
+                        total += rx[q, j, tile].astype(F32)
+                    lo = mine + part.lo + part.ring[0] * part.one + part.own
+                    rows = span(lo, part.tile)
+                    out[rows] = total.astype(BF16)
+                    for t, column in enumerate(place.lines[part.second]):
+                        for d, other in enumerate(z_ring):
+                            if t or d:
+                                send(6 + part.p, out.at[rows], out.at[rows], (column, other))
+
+        def chunk(part, i, skip=0, rows=None):
+            return span(mine + part.lo + i * part.one + skip, part.one if rows is None else rows)
+
+        def step_ring():
             for part in parts:
-                rows = chunk(part, spot[part.first], spot[part.second])
-                out[rows] = zt[q, part.kept : part.kept + part.two]
-                spread(8 + part.p, rows, part.second, False)
-
-        def deliver(rows):
-            send(10, out.at[rows], home.at[rows], mate)
-
-        def step_six():
-            for part in parts:
-                arrived(8 + part.p, (s.size[part.second] - 1) * part.two)
-                rows = chunk(part, spot[part.first])
-                spread(11 + 3 * part.p, rows, part.first, True)
-            if len(parts) > 1:
-                for part in parts:
-                    deliver(chunk(part, spot[part.first]))
+
+                @pl.when(part.owner)
+                def _(part=part):
+                    arrived(6 + part.p, part.one - part.tile)
+
+                @pl.when(jnp.logical_not(part.owner))
+                def _(part=part):
+                    arrived(6 + part.p, part.one)
+
+                rows = chunk(part, part.ring[0])
+                for d in (1, 3) if relay else range(1, part.n):
+                    send(8 + part.p, out.at[rows], out.at[rows], (part.line[d], z))
+
+        def step_relay_back():
+            (part,) = parts
+            half = part.one // 2
+            arrived(8, 2 * part.one)
+            rows = chunk(part, part.ring[3], 0, half)
+            send(9, out.at[rows], out.at[rows], (part.line[1], z))
+            rows = chunk(part, part.ring[1], half, half)
+            send(9, out.at[rows], out.at[rows], (part.line[3], z))
 
         def keep():
             return pltpu.make_async_copy(
                 out.at[span(mine, s.half)], home.at[span(mine, s.half)], store_sem.at[6 + q]
             )
 
-        def step_seven():
-            for d in (1, 3, 2):
-                for part in parts:
-                    n = s.size[part.first]
-                    if d < n:
-                        arrived(11 + 3 * part.p + d - 1, part.one)
-                        if len(parts) > 1:
-                            deliver(chunk(part, place.rings[part.first][n - d]))
-            if len(parts) == 1:
-                deliver(span(mine, s.half))
+        def step_deliver():
+            for part in parts:
+                if relay:
+                    arrived(9, part.one)
+                else:
+                    arrived(8 + part.p, (part.n - 1) * part.one)
+                rows = span(mine + part.lo, part.n * part.one)
+                send(16, out.at[rows], home.at[rows], mate)
             keep().start()
 
-        def step_eight():
-            arrived(10, s.half)
+        def step_end():
+            arrived(16, s.half)
             keep().wait()
 
         def finish():
             sent(0, 9 * C)
             sent(1, 5 * C)
+            sent(16, s.half)
             for part in parts:
-                first, second = s.size[part.first], s.size[part.second]
-                sent(2 + part.p, (first - 1) * part.one)
-                sent(4 + part.p, (second - 1) * part.two)
-                sent(8 + part.p, (second - 1) * part.two)
-                for d in range(1, first):
-                    sent(11 + 3 * part.p + d - 1, part.one)
-            sent(6, (s.nz - 1) * s.z_rows)
-            sent(7, (s.nz - 1) * s.z_rows)
-            sent(10, s.half)
-
-        return [
-            None,
-            step_one,
-            step_two,
-            step_three,
-            step_four,
-            step_five,
-            step_six,
-            step_seven,
-            step_eight,
-            finish,
-        ]
+                if relay:
+                    sent(2, part.one)
+                    sent(3, 2 * part.one)
+                    sent(8, 2 * part.one)
+                    sent(9, part.one)
+                else:
+                    sent(2 + part.p, (part.n - 1) * part.one)
+                    sent(8 + part.p, (part.n - 1) * part.one)
+
+                @pl.when(part.owner)
+                def _(part=part):
+                    sent(4 + part.p, part.one - part.tile)
+                    sent(6 + part.p, (plane - 1) * part.tile)
+
+                @pl.when(jnp.logical_not(part.owner))
+                def _(part=part):
+                    sent(4 + part.p, part.one)
+
+        if relay:
+            steps = [step_mate, step_relay, step_plane, step_own, step_ring, step_relay_back]
+        else:
+            steps = [step_mate, step_plane, step_own, step_ring]
+        return steps + [step_deliver, step_end, finish]
 
     def store(i, src, dst):
         copy = pltpu.make_async_copy(src, dst, store_sem.at[i])
@@ -605,86 +639,84 @@
     place.halo_start(0, xe, True)
     loads[1].wait()
     place.halo_start(1, ue, False)
-    place.stats_stage(0, 0)
     for load in loads[2:]:
         load.wait()
     gain1, shift1, gain2, shift2 = (vectors[i] for i in range(4))
-    place.stats_stage(0, 1)
+    turn(w2_ref, wf2)
+    place.stats_stage(0, 0)
+    turn(w1_ref, wf1)
     place.halo_wait(0, xe)
     copy_first(place, xe)
-    place.halo_wait(1, ue)
-    blank_next(place, ue)
-    stats1 = place.stats_stage(0, 2)
+    stats1 = place.stats_stage(0, 1)
 
     build_act(xe, a1, stats1, gain1, shift1)
-    for f, value in enumerate(conv(a1, w1_ref)):
+    for f, value in enumerate(conv(a1, taps_of(w1_ref))):
         he[2 + f, 1 : R + 1] = value.astype(BF16).reshape(R, W, C)
     hidden = place.own_block(he, 2)
     place.ar_start(1, 0, place.local_stats(place.own(hidden)))
+    place.halo_wait(1, ue)
+    blank_next(place, ue)
     build_grad(ue)
     place.stats_stage(1, 0)
     place.halo_start(2, he, True)
-    back_conv(g3, w2_ref)
-    place.stats_stage(1, 1)
+    back_conv(g3, wf2)
+    back_first(g3, wf2)
     place.halo_wait(2, he)
     copy_first(place, he)
-    stats2 = place.stats_stage(1, 2)
-
-    second = weight_reduce(1, wo2_hbm, arrivals[4:])
-    first = weight_reduce(0, wo1_hbm, arrivals[:4])
+    stats2 = place.stats_stage(1, 1)
+
+    second = iter(weight_sum(1, wo2_hbm, arrivals[2:], True))
+    first = iter(weight_sum(0, wo1_hbm, arrivals[:2], False))
     place.ar_start(2, 0, norm_back_sums(hidden, stats2, gain2, shift2))
     build_act(he, a2, stats2, gain2, shift2)
     place.sums_stage(2, 0)
     weight_grad(a2, u_ref, 1)
-    place.sums_stage(2, 1)
-    second[1]()
-    sums2 = place.sums_stage(2, 2)
+    sums2 = place.sums_stage(2, 1)
     for f in range(F):
         value = norm_back_value(hidden, stats2, gain2, sums2, f)
         ge[f, 1 : R + 1] = value.astype(BF16).reshape(R, W, C)
     place.halo_start(3, ge, False)
+    next(second)()
     weight_grad(a1, place.own_block(ge, 0), 0)
-    first[1]()
-    second[2]()
+    next(second)()
+    next(first)()
     place.halo_wait(3, ge)
     blank_next(place, ge)
     build_grad(ge)
-    back_conv(g3, w1_ref)
+    next(second)()
+    back_conv(g3, wf1)
+    back_first(g3, wf1)
     place.ar_start(3, 0, norm_back_sums(x_ref, stats1, gain1, shift1))
-    first[2]()
-    second[3]()
-    place.sums_stage(3, 0)
-    branch = conv(a2, w2_ref)
-    first[3]()
-    place.sums_stage(3, 1)
+    next(first)()
+    next(second)()
+    branch = conv(a2, taps_of(w2_ref))
     for f in range(F):
         total = x_ref[f].astype(F32).reshape(cells, C) + branch[f]
         out_ref[f] = total.astype(BF16).reshape(R, W, C)
     stores = [store(0, out_ref, out_hbm)]
-    second[4]()
-    first[4]()
-    sums1 = place.sums_stage(3, 2)
-    second[5]()
-    first[5]()
+    next(first)()
+    place.sums_stage(3, 0)
+    next(second)()
+    next(first)()
+    next(second)()
+    sums1 = place.sums_stage(3, 1)
     for f in range(F):
         value = norm_back_value(x_ref, stats1, gain1, sums1, f)
         total = u_ref[f].astype(F32).reshape(cells, C) + value
         ig_ref[f] = total.astype(BF16).reshape(R, W, C)
     stores.append(store(1, ig_ref, ig_hbm))
-    second[6]()
-    first[6]()
     for i, (row, result) in enumerate(zip(sums1 + sums2, (gg1_hbm, sg1_hbm, gg2_hbm, sg2_hbm))):
         results[i] = row
         stores.append(store(2 + i, results.at[i], result))
-    second[7]()
-    first[7]()
-    second[8]()
-    first[8]()
+    next(second)()
+    next(first)()
+    next(second)()
+    next(first)()
 
     for copy in stores:
         copy.wait()
-    second[9]()
-    first[9]()
+    next(second)()
+    next(first)()
     for k in range(4):
         place.ar_sent(k)
     for q, ref in enumerate((xe, ue, he, ge)):
@@ -745,11 +777,11 @@
     wide = pltpu.VMEM((E, RE, W, C), BF16)
     wider = pltpu.VMEM((E, RE, W, 3 * C), BF16)
     arrivals = []
-    for parts in s.parts:
-        for first, second, rows in parts:
-            one = rows // s.size[first]
-            arrivals.append(pltpu.VMEM((s.size[first], one, C), BF16))
-            arrivals.append(pltpu.VMEM((s.size[second], one // s.size[second], C), BF16))
+    for first, _, rows, _, _ in s.parts[0]:
+        arrivals.append(pltpu.VMEM((s.size[first], rows // s.size[first], C), BF16))
+    ((first, _, rows, _, _),) = s.parts[1]
+    arrivals.append(pltpu.VMEM((2, rows // s.size[first] // 2, C), BF16))
+    arrivals.append(pltpu.VMEM((2, rows // s.size[first], C), BF16))
     room = 60 * 1024 * 1024
     results = pl.pallas_call(
         functools.partial(kernel, s),
@@ -759,6 +791,8 @@
         scratch_shapes=[
             pltpu.VMEM((27, C, C), BF16),
             pltpu.VMEM((27, C, C), BF16),
+            pltpu.VMEM((3, 9 * C, C), BF16),
+            pltpu.VMEM((3, 9 * C, C), BF16),
             pltpu.VMEM((4, 1, C), F32),
             pltpu.VMEM((F, R, W, C), BF16),
             pltpu.VMEM((F, R, W, C), BF16),
@@ -773,16 +807,14 @@
             wider,
             pltpu.VMEM((F, cells, C), F32),
             pltpu.VMEM((F, cells, C), F32),
-            pltpu.VMEM((12, max(s.stages), 2, C), F32),
+            pltpu.VMEM((8, max(s.stages), 2, C), F32),
             pltpu.VMEM((2, s.taps * C, C), BF16),
             pltpu.VMEM((2, s.half, C), BF16),
             pltpu.VMEM((2, s.half, C), BF16),
-            pltpu.VMEM((2, s.nz * s.z_rows, C), BF16),
-            pltpu.VMEM((2, s.nz, s.z_rows, C), BF16),
-            pltpu.VMEM((2, s.nz * s.z_rows, C), BF16),
+            pltpu.VMEM((2, 4 * s.nz, s.tile, C), BF16),
             arrivals,
-            pltpu.SemaphoreType.DMA((12,)),
-            pltpu.SemaphoreType.DMA((12,)),
+            pltpu.SemaphoreType.DMA((8,)),
+            pltpu.SemaphoreType.DMA((8,)),
             pltpu.SemaphoreType.DMA((4,)),
             pltpu.SemaphoreType.DMA((4,)),
             pltpu.SemaphoreType.DMA((2, 17)),

time: 85.1 us -> 82.1 us (0.965)
  Pallas kernels: 84.3 us -> 81.4 us
    pallas_call x1, Pallas kernels: 81 us -> 78.1 us  [body(): pl.pallas_call(functools.partial(kernel, s), out_shape=[field, field, wei...]
where the time goes in v3:
time: 82.1 us; the launch traced here: 82 us
  Pallas kernels  81.4 us (99%)
    pallas_call x1, Pallas kernels, body(): pl.pallas_call(functools.partial(kernel, s), out_shape=[field, field, wei...  78.1 us
    pallas_call x1, Pallas kernels, body(): pl.pallas_call(finish_kernel, out_shape=[field, field, total, total, vect...  3.26 us

profile of v3, /device:TPU:1, one launch (start us, length us, event | category | flops | bytes accessed | tf_op | source)
XLA Modules:
  0.0 82.0 jit_solution(8448470616093067117)
XLA Ops:
  0.6 78.1 %shard_map.143 = (bf16[2,4,64,128]{3,2,1,0:T(8,128)(2,1)}, bf16[2,4,64,128]{3,2,1,0:T(8,128)(2,1)}, bf16[3584,128]{1,0:T(8,128)(2,1)}, bf16[3584,128]{1,0:T(8,12...) custom-call(bf16[2,4,64,128]{3,2,1,0:T(8,128)(2,1)} %x_hbm.1, ...), custom_call_target="tpu_custom_call" | custom-call | flops 2717908992 | bytes 8000000 | tf_op jit(solution)/shard_map/pallas_call | solution.py:786
  78.7 3.3 %shard_map.144 = (bf16[2,4,64,128]{3,2,1,0:T(8,128)(2,1)}, bf16[2,4,64,128]{3,2,1,0:T(8,128)(2,1)}, f32[3456,128]{1,0:T(8,128)}, f32[3456,128]{1,0:T(8,128)}, f3...) custom-call(bf16[2,4,64,128]{3,2,1,0:T(8,128)(2,1)} %get-tuple-element.24.refs_0_, ...), custom_call_target="tpu_custom_call" | custom-call | bytes 6000000 | tf_op jit(solution)/shard_map/pallas_call | solution.py:842

commit v4 on v3

--- a/solution.py
+++ b/solution.py
@@ -384,7 +384,7 @@
                 for k in range(3):
                     at = 3 * i + k
                     lo = base(at) * C
-                    wg[q, pl.ds(pl.multiple_of(lo, C), C), :] = total[:, k * C : (k + 1) * C].T
+                    wg[q, pl.ds(pl.multiple_of(lo, C), C), :] = total[:, k * C : (k + 1) * C]
 
         def send(i, src, dst, taps):
             pltpu.make_async_remote_copy(
@@ -683,22 +683,19 @@
     place.halo_wait(3, ge)
     blank_next(place, ge)
     build_grad(ge)
-    next(second)()
     back_conv(g3, wf1)
     back_first(g3, wf1)
     place.ar_start(3, 0, norm_back_sums(x_ref, stats1, gain1, shift1))
+    next(second)()
     next(first)()
-    next(second)()
     branch = conv(a2, taps_of(w2_ref))
     for f in range(F):
         total = x_ref[f].astype(F32).reshape(cells, C) + branch[f]
         out_ref[f] = total.astype(BF16).reshape(R, W, C)
     stores = [store(0, out_ref, out_hbm)]
-    next(first)()
     place.sums_stage(3, 0)
     next(second)()
     next(first)()
-    next(second)()
     sums1 = place.sums_stage(3, 1)
     for f in range(F):
         value = norm_back_value(x_ref, stats1, gain1, sums1, f)
@@ -712,6 +709,9 @@
     next(first)()
     next(second)()
     next(first)()
+    next(second)()
+    next(first)()
+    next(second)()
 
     for copy in stores:
         copy.wait()
@@ -754,7 +754,7 @@
                     at = 3 * i + k
                     tap = lo + at + (1 if count == 10 and at >= 5 else 0)
                     block = narrow[q, tap * C : (tap + 1) * C]
-                    wide[q, to + k * C : to + (k + 1) * C] = block.astype(F32)
+                    wide[q, to + k * C : to + (k + 1) * C] = block.T.astype(F32)
                 rows = pl.ds(to, 3 * C)
                 write(wide.at[q, rows], places[2 + q].at[rows])
         if j == 0:

time: 82.1 us -> 82.2 us (level)
  no operation moved by 1% of the time
where the time goes in v4:
time: 82.2 us; the launch traced here: 82.1 us
  Pallas kernels  81.4 us (99%)
    pallas_call x1, Pallas kernels, body(): pl.pallas_call(functools.partial(kernel, s), out_shape=[field, field, wei...  78.1 us
    pallas_call x1, Pallas kernels, body(): pl.pallas_call(finish_kernel, out_shape=[field, field, total, total, vect...  3.3 us

profile of v4, /device:TPU:1, one launch (start us, length us, event | category | flops | bytes accessed | tf_op | source)
XLA Modules:
  0.0 82.1 jit_solution(4530685044203879774)
XLA Ops:
  0.6 78.1 %shard_map.143 = (bf16[2,4,64,128]{3,2,1,0:T(8,128)(2,1)}, bf16[2,4,64,128]{3,2,1,0:T(8,128)(2,1)}, bf16[3584,128]{1,0:T(8,128)(2,1)}, bf16[3584,128]{1,0:T(8,12...) custom-call(bf16[2,4,64,128]{3,2,1,0:T(8,128)(2,1)} %x_hbm.1, ...), custom_call_target="tpu_custom_call" | custom-call | flops 2717908992 | bytes 8000000 | tf_op jit(solution)/shard_map/pallas_call | solution.py:786
  78.8 3.3 %shard_map.144 = (bf16[2,4,64,128]{3,2,1,0:T(8,128)(2,1)}, bf16[2,4,64,128]{3,2,1,0:T(8,128)(2,1)}, f32[3456,128]{1,0:T(8,128)}, f32[3456,128]{1,0:T(8,128)}, f3...) custom-call(bf16[2,4,64,128]{3,2,1,0:T(8,128)(2,1)} %get-tuple-element.24.refs_0_, ...), custom_call_target="tpu_custom_call" | custom-call | bytes 6000000 | tf_op jit(solution)/shard_map/pallas_call | solution.py:842

commit v5 on v4

--- a/solution.py
+++ b/solution.py
@@ -696,6 +696,7 @@
     place.sums_stage(3, 0)
     next(second)()
     next(first)()
+    next(second)()
     sums1 = place.sums_stage(3, 1)
     for f in range(F):
         value = norm_back_value(x_ref, stats1, gain1, sums1, f)
@@ -705,7 +706,6 @@
     for i, (row, result) in enumerate(zip(sums1 + sums2, (gg1_hbm, sg1_hbm, gg2_hbm, sg2_hbm))):
         results[i] = row
         stores.append(store(2 + i, results.at[i], result))
-    next(second)()
     next(first)()
     next(second)()
     next(first)()

time: 82.2 us -> 82.2 us (level)
  no operation moved by 1% of the time
where the time goes in v5:
time: 82.2 us; the launch traced here: 82.1 us
  Pallas kernels  81.4 us (99%)
    pallas_call x1, Pallas kernels, body(): pl.pallas_call(functools.partial(kernel, s), out_shape=[field, field, wei...  78.1 us
    pallas_call x1, Pallas kernels, body(): pl.pallas_call(finish_kernel, out_shape=[field, field, total, total, vect...  3.3 us

profile of v5, /device:TPU:1, one launch (start us, length us, event | category | flops | bytes accessed | tf_op | source)
XLA Modules:
  0.0 82.1 jit_solution(7489267669464541644)
XLA Ops:
  0.6 78.1 %shard_map.143 = (bf16[2,4,64,128]{3,2,1,0:T(8,128)(2,1)}, bf16[2,4,64,128]{3,2,1,0:T(8,128)(2,1)}, bf16[3584,128]{1,0:T(8,128)(2,1)}, bf16[3584,128]{1,0:T(8,12...) custom-call(bf16[2,4,64,128]{3,2,1,0:T(8,128)(2,1)} %x_hbm.1, ...), custom_call_target="tpu_custom_call" | custom-call | flops 2717908992 | bytes 8000000 | tf_op jit(solution)/shard_map/pallas_call | solution.py:786
  78.8 3.3 %shard_map.144 = (bf16[2,4,64,128]{3,2,1,0:T(8,128)(2,1)}, bf16[2,4,64,128]{3,2,1,0:T(8,128)(2,1)}, f32[3456,128]{1,0:T(8,128)}, f32[3456,128]{1,0:T(8,128)}, f3...) custom-call(bf16[2,4,64,128]{3,2,1,0:T(8,128)(2,1)} %get-tuple-element.24.refs_0_, ...), custom_call_target="tpu_custom_call" | custom-call | bytes 6000000 | tf_op jit(solution)/shard_map/pallas_call | solution.py:842
